TPU v7x, 32 devices: a whole 2x2x4 slice. The times are simulated.
32 devices in a mesh: region: 8 (over z, y), local: 4 (over x, core).
Axes of the slice: x: 2, y: 2, z: 4, core: 2. Of those that a mesh axis runs over, the one named last changes fastest.
Arguments:
- atm_flux: bfloat16 [12, 131072], P(None, ('region', 'local')), may hold values from -6 to 6
- cell_map: int32 [32, 4096], P(('region', 'local')), may hold values from 0 to 4095, each once within a row
- neighbours: int32 [4, 131072], P(None, ('region', 'local')), may hold values from 0 to 4095
- coef_x: float32 [4, 131072], P(None, ('region', 'local')), may hold values from -3 to 3
- coef_y: float32 [4, 131072], P(None, ('region', 'local')), may hold values from -3 to 3
- send_list: int32 [32, 4, 4], P(('region', 'local')), may hold values from 0 to 31, as said below
- cover: int32 [128, 4], P(('region', 'local')), may hold values from 0 to 15, as said below
- cover_count: int32 [128], P(('region', 'local')), may hold values from 1 to 4
- weights: bfloat16 [128, 4, 3, 128, 128], P(('region', 'local')), may hold values from -0.15625 to 0.15625
- ocean_map: int32 [32, 512], P(('region', 'local')), may hold values from 0 to 511, each once within a row
Outputs:
- ocean_flux: float32 [12, 16384], P(None, ('region', 'local'))
Inputs may be any that keep to these rules, and one draw needn't show every extreme that they name: `cell_map`: each row is a permutation of one device's cells. `neighbours`: indices of coupler cells on the same device. `send_list`: each row lists 4 different source blocks of the sending device. `cover`: each row lists 4 different slots of what the owner receives from its region. `ocean_map`: each row is a permutation of one device's ocean cells.
All inputs are finite; a program needn't handle non-finite values.
Results may differ from a plain program's by a relative error of at most 0.0024.
Values may be sent and summed in bfloat16 or wider, within the bound.
No kernel may reach another device: no remote copies, remote signals or barrier semaphores. Data moves between devices by JAX's collectives and lax.ppermute only.
A program may use at most 64 MiB of HBM per device.

v0:
```python
import jax
import jax.numpy as jnp
from jax import lax
from jax.sharding import PartitionSpec as P


def reconstruct(values, near_index, weight_x, weight_y):
    nearby = values[:, near_index]
    change = nearby - values[:, None, :]
    slope_x = jnp.sum(weight_x[None] * change, axis=1)
    slope_y = jnp.sum(weight_y[None] * change, axis=1)
    upper = jnp.maximum(values, jnp.max(nearby, axis=1))
    lower = jnp.minimum(values, jnp.min(nearby, axis=1))
    steep = jnp.abs(slope_x) + jnp.abs(slope_y)
    factor = jnp.minimum(1.0, (upper - lower) / jnp.maximum(steep, 1.0))
    return jnp.stack([values, factor * slope_x, factor * slope_y]).astype(jnp.bfloat16)


def shards(
    atm_flux,
    cell_map,
    neighbours,
    coef_x,
    coef_y,
    send_list,
    cover,
    cover_count,
    weights,
    ocean_map,
):
    fields, cells = atm_flux.shape
    region_count = lax.axis_size("region")
    local_count = lax.axis_size("local")
    piece = cells // (region_count * local_count)
    outgoing = atm_flux[:, cell_map[0]].reshape(fields, region_count, local_count, piece)
    arrived = lax.all_to_all(
        lax.all_to_all(outgoing, "region", split_axis=1, concat_axis=1, tiled=True),
        "local",
        split_axis=2,
        concat_axis=2,
        tiled=True,
    )
    coupled = arrived.reshape(fields, cells).astype(jnp.float32)
    recon = reconstruct(coupled, neighbours, coef_x, coef_y)
    block_size = weights.shape[-1]
    block_count = cells // block_size
    recon = recon.reshape(3, fields, block_count, block_size)
    pooled, lists = (
        lax.all_gather(recon, "local", axis=2, tiled=True),
        lax.all_gather(send_list, "local", axis=0, tiled=True),
    )
    member = lax.axis_index("local")
    wanted = lax.dynamic_index_in_dim(lists, member, 1, keepdims=False)
    offsets = jnp.arange(local_count, dtype=jnp.int32)[:, None] * block_count
    flat_index = (wanted + offsets).reshape(-1)
    source = pooled[:, :, flat_index]
    chosen = source[:, :, cover]
    slot_total = cover.shape[1]
    live = (jnp.arange(slot_total, dtype=jnp.int32)[None, :] < cover_count[:, None]).astype(
        jnp.bfloat16
    )
    chosen = chosen * live[None, None, :, :, None]
    remapped = jnp.einsum("bkmos,mfbks->fbo", weights, chosen, preferred_element_type=jnp.float32)
    coupler_out = remapped.reshape(fields, -1)
    ocean_cells = coupler_out.shape[1]
    leaving = coupler_out[:, ocean_map[0]].reshape(
        fields, region_count, ocean_cells // region_count
    )
    landed = lax.all_to_all(leaving, "region", split_axis=1, concat_axis=1, tiled=True)
    return landed.reshape(fields, ocean_cells)


def solution(mesh):
    return jax.shard_map(
        shards,
        mesh=mesh,
        in_specs=(
            P(None, ("region", "local")),
            P(("region", "local"), None),
            P(None, ("region", "local")),
            P(None, ("region", "local")),
            P(None, ("region", "local")),
            P(("region", "local"), None, None),
            P(("region", "local"), None),
            P(("region", "local")),
            P(("region", "local"), None, None, None, None),
            P(("region", "local"), None),
        ),
        out_specs=P(None, ("region", "local")),
        check_vma=False,
    )
```

profile of v0, /device:TPU:0, one launch (start us, length us, event | category | flops | bytes accessed | tf_op | source)
XLA Modules:
  0.0 170.0 jit_solution(8442352189152640065)
XLA Ops:
  6.5 0.0 copy-start
  6.5 0.0 copy-start.3
  6.5 1.5 copy.82
  8.1 0.7 compare_select_fusion.1
  8.8 14.9 %gather_fusion = bf16[4096,12]{1,0:T(8,128)(2,1)} fusion(bf16[12,4096]{0,1:T(8,128)(2,1)S(1)} %copy.82, s32[4096]{0:T(1024)S(1)} %broadcast_clamp_fusion.1), kind=kCustom, calls=%fused_computation | custom fusion | bytes 212992 | tf_op jit(solution)/shard_map/gather | solution.py:35
  23.7 2.3 %copy.83 = bf16[12,8,4,128]{3,2,0,1:T(4,128)(2,1)} copy(bf16[12,8,4,128]{0,3,2,1:T(8,128)(2,1)} %bitcast.47) | data formatting | bytes 196608 | tf_op jit(solution)/shard_map/reshape | solution.py:35
  26.0 7.3 %all-to-all-start = ((bf16[12,8,4,128]{3,2,0,1:T(4,128)(2,1)}), bf16[12,8,4,128]{3,2,0,1:T(4,128)(2,1)S(1)}, u32[]{:S(2)}, u32[]{:S(2)}) async-start(bf16[12,8,4,128]{3,2,0,1:T(4,128)(2,1)} %copy.83), calls=%async_computation | async-start | bytes 196608 | tf_op jit(solution)/shard_map/all_to_all | solution.py:37
  33.3 0.0 copy-done.3
  33.3 7.1 %all-to-all-done = bf16[12,8,4,128]{3,2,0,1:T(4,128)(2,1)S(1)} async-done(((bf16[12,8,4,128]{3,2,0,1:T(4,128)(2,1)}), bf16[12,8,4,128]{3,2,0,1:T(4,128)(2,1)S(1)}, u32[]{:S(2)}, u32[]{:S(2)}) %all-to-all-start) | async-done | bytes 98336 | tf_op jit(solution)/shard_map/all_to_all | solution.py:37
  40.4 0.6 copy.84
  41.0 3.3 %all-to-all-start.1 = ((bf16[12,8,4,128]{3,1,0,2:T(8,128)(2,1)}), bf16[12,8,4,128]{3,1,0,2:T(8,128)(2,1)S(1)}, u32[]{:S(2)}, u32[]{:S(2)}) async-start(bf16[12,8,4,128]{3,1,0,2:T(8,128)(2,1)} %copy.84), calls=%async_computation.1 | async-start | bytes 196608 | tf_op jit(solution)/shard_map/all_to_all | solution.py:36
  44.3 0.0 all-gather.2.cloned.1.call-start
  44.4 4.2 %all-to-all-done.1 = bf16[12,8,4,128]{3,1,0,2:T(8,128)(2,1)S(1)} async-done(((bf16[12,8,4,128]{3,1,0,2:T(8,128)(2,1)}), bf16[12,8,4,128]{3,1,0,2:T(8,128)(2,1)S(1)}, u32[]{:S(2)}, u32[]{:S(2)}) %all-to-all-start.1) | async-done | bytes 98336 | tf_op jit(solution)/shard_map/all_to_all | solution.py:36
  48.6 1.8 %copy.86 = f32[12,8,4,128]{0,3,2,1:T(8,128)} copy(bf16[12,8,4,128]{3,1,0,2:T(8,128)(2,1)S(1)} %all-to-all-done.1) | data formatting | bytes 294912 | tf_op jit(solution)/shard_map/convert_element_type | solution.py:43
  50.4 0.0 copy-start.1
  50.4 0.0 copy-start.2
  50.4 56.0 %gather_fusion.1 = f32[16384,12]{1,0:T(8,128)} fusion(f32[12,4096]{0,1:T(8,128)} %bitcast.40, s32[16384]{0:T(1024)S(1)} %broadcast_clamp_fusion), kind=kCustom, calls=%fused_computation.1 | custom fusion | bytes 1638400 | tf_op jit(solution)/shard_map/gather | solution.py:8
  106.5 0.0 copy-done.1
  106.5 0.0 copy-done.2
  106.5 13.1 %fusion.13 = (f32[12,4096]{0,1:T(8,128)}, f32[12,4096]{0,1:T(8,128)}, f32[12,4096]{0,1:T(8,128)}, f32[12,4096]{0,1:T(8,128)}) fusion(f32[12,4,4096]{0,2,1:T(8,128)} %bitcast.42, f32[12,4096]{0,1:T(8,128)} %bitcast.41, f32[4,4096]{1,0:T(4,128)S(1)} %copy-done.1, f32[4,4096]{1,0:T(4,128)S(1)} %copy-done.2), kind=kLoop, calls=%fused_computation.37 | loop fusion | flops 1179648 | bytes 1900544 | tf_op jit(solution)/shard_map/reduce_max | solution.py:12
  119.5 2.2 %copy.100 = f32[1,12,32,128]{3,2,1,0:T(8,128)S(1)} copy(f32[1,12,32,128]{1,3,2,0:T(8,128)} %bitcast.46) | data formatting | bytes 393216 | tf_op jit(solution)/shard_map/reduce_max | solution.py:12
  121.8 2.2 %copy.101 = f32[1,12,32,128]{3,2,1,0:T(8,128)S(1)} copy(f32[1,12,32,128]{1,3,2,0:T(8,128)} %bitcast.45) | data formatting | bytes 393216 | tf_op jit(solution)/shard_map/reduce_min | solution.py:13
  124.0 2.2 %copy.102 = f32[1,12,32,128]{3,2,1,0:T(8,128)S(1)} copy(f32[1,12,32,128]{1,3,2,0:T(8,128)} %bitcast.44) | data formatting | bytes 393216 | tf_op jit(solution)/shard_map/reduce_sum | solution.py:10
  126.2 0.0 copy-start.4
  126.2 0.0 copy-start.5
  126.3 0.0 copy-start.6
  126.3 0.0 copy-start.7
  126.3 2.2 %copy.103 = f32[1,12,32,128]{3,2,1,0:T(8,128)S(1)} copy(f32[1,12,32,128]{1,3,2,0:T(8,128)} %bitcast.43) | data formatting | bytes 393216 | tf_op jit(solution)/shard_map/reduce_sum | solution.py:11
  128.5 0.1 copy.85
  128.6 0.1 multiply_convert_fusion.1
  128.7 0.8 pad_maximum_fusion
  129.5 0.0 all-gather.2.cloned.1.call-update
  129.5 0.0 copy-done.4
  129.5 5.2 %all_gather.7 = s32[4,4,4]{2,1,0:T(4,128)S(1)} all-gather(s32[1,4,4]{2,1,0:T(4,128)S(1)} %copy-done.4), channel_id=1, replica_groups=mesh['region'=8,'local'=4] {'local'}, dimensions={0}, use_global_device_ids=true | all-gather | bytes 320 | tf_op jit(solution)/shard_map/all_gather | solution.py:50
  134.7 0.1 squeeze.11
  134.8 0.1 add.89
  134.9 0.1 add.90
  135.0 0.0 copy-done.5
  135.0 0.1 reshape.281
  135.1 0.0 copy-done.6
  135.1 0.0 copy-done.7
  135.1 8.7 %all-gather.2.cloned.1.call-done = bf16[3,12,128,128]{3,2,1,0:T(8,128)(2,1)} async-done(((bf16[3,12,32,128]{3,2,1,0:T(8,128)(2,1)}), bf16[3,12,128,128]{3,2,1,0:T(8,128)(2,1)}) %all-gather.2.cloned.1.call-update) | async-done | bytes 1179664 | tf_op jit(solution)/shard_map/all_gather | solution.py:49
  143.8 2.1 %copy.91 = bf16[3,12,128,128]{3,1,2,0:T(8,128)(2,1)S(1)} copy(bf16[3,12,128,128]{3,2,1,0:T(8,128)(2,1)} %all-gather.2.cloned.1.call-done) | data formatting | bytes 2359296 | tf_op jit(solution)/shard_map/all_gather | solution.py:49
  145.9 0.6 gather_fusion.2
  146.5 0.6 gather_fusion.3
  147.2 0.0 copy-done
  147.2 0.5 fusion.2
  147.7 0.2 copy.104
  147.9 1.0 gather_fusion.4
  148.9 0.1 copy.97
  149.1 0.1 reshape.307
  149.2 11.9 %all_to_all.15 = f32[8,1,768]{2,1,0:T(1,128)S(1)} all-to-all(f32[8,1,768]{2,1,0:T(1,128)S(1)} %reshape.307), channel_id=1, replica_groups=mesh['region'=8,'local'=4] {'region'}, dimensions={0} | all-to-all | bytes 49152 | tf_op jit(solution)/shard_map/all_to_all | solution.py:69
  161.1 0.5 broadcast.152
  161.6 0.7 reduce.6
  162.3 0.1 reshape.308
  162.4 0.7 reshape.253
  (15 shorter events, 0.1 us)
Async XLA Ops:
  6.5 140.6 %copy-start = (bf16[4,4,3,128,128]{4,3,2,1,0:T(8,128)(2,1)S(1)}, bf16[4,4,3,128,128]{4,3,2,1,0:T(8,128)(2,1)}, u32[]{:S(2)}) copy-start(bf16[4,4,3,128,128]{4,3,2,1,0:T(8,128)(2,1)} %param.18) | copy-start | bytes 4718596
  6.5 26.7 %copy-start.3 = (s32[4,4096]{1,0:T(4,128)S(1)}, s32[4,4096]{1,0:T(4,128)}, u32[]{:S(2)}) copy-start(s32[4,4096]{1,0:T(4,128)} %param.12) | copy-start | bytes 196612
  26.0 14.4 %all-to-all-start = ((bf16[12,8,4,128]{3,2,0,1:T(4,128)(2,1)}), bf16[12,8,4,128]{3,2,0,1:T(4,128)(2,1)S(1)}, u32[]{:S(2)}, u32[]{:S(2)}) async-start(bf16[12,8,4,128]{3,2,0,1:T(4,128)(2,1)} %copy.83), calls=%async_computation | async-start | bytes 196608 | tf_op jit(solution)/shard_map/all_to_all | solution.py:37
  41.0 7.6 %all-to-all-start.1 = ((bf16[12,8,4,128]{3,1,0,2:T(8,128)(2,1)}), bf16[12,8,4,128]{3,1,0,2:T(8,128)(2,1)S(1)}, u32[]{:S(2)}, u32[]{:S(2)}) async-start(bf16[12,8,4,128]{3,1,0,2:T(8,128)(2,1)} %copy.84), calls=%async_computation.1 | async-start | bytes 196608 | tf_op jit(solution)/shard_map/all_to_all | solution.py:36
  44.3 99.5 %all-gather.2.cloned.1.call-start = ((), (), s32[]{:S(2)}) async-start(), calls=%async_computation.3 | async-start | bytes 1474560 | tf_op jit(solution)/shard_map/all_gather | solution.py:49
  50.4 56.0 %copy-start.1 = (f32[4,4096]{1,0:T(4,128)S(1)}, f32[4,4096]{1,0:T(4,128)}, u32[]{:S(2)}) copy-start(f32[4,4096]{1,0:T(4,128)} %param.14) | copy-start | bytes 196612
  50.4 56.0 %copy-start.2 = (f32[4,4096]{1,0:T(4,128)S(1)}, f32[4,4096]{1,0:T(4,128)}, u32[]{:S(2)}) copy-start(f32[4,4096]{1,0:T(4,128)} %param.13) | copy-start | bytes 196612
  126.2 3.3 %copy-start.4 = (s32[1,4,4]{2,1,0:T(4,128)S(1)}, s32[1,4,4]{2,1,0:T(4,128)}, u32[]{:S(2)}) copy-start(s32[1,4,4]{2,1,0:T(4,128)} %param.15) | copy-start | bytes 196
  126.2 8.7 %copy-start.5 = (s32[4,4]{1,0:T(4,128)S(1)}, s32[4,4]{1,0:T(4,128)}, u32[]{:S(2)}) copy-start(s32[4,4]{1,0:T(4,128)} %param.16) | copy-start | bytes 196
  126.3 8.8 %copy-start.6 = (s32[1,512]{1,0:T(1,128)S(1)}, s32[1,512]{1,0:T(1,128)}, u32[]{:S(2)}) copy-start(s32[1,512]{1,0:T(1,128)} %param.19) | copy-start | bytes 6148
  126.3 8.8 %copy-start.7 = (s32[4]{0:T(128)S(1)}, s32[4]{0:T(128)}, u32[]{:S(2)}) copy-start(s32[4]{0:T(128)} %param.17) | copy-start | bytes 52
Sparse Core Ops, SparseCore 0:
  129.6 14.1 all-gather.1
where the time goes:
time: 171 us; the launch traced here: 170 us
  local copies, waits for them, and re-layouts  92.6 us (54%)
  waiting for transfers between devices  20 us (12%)
  blocking collectives  17.1 us (10%)
  other arithmetic  15.5 us (9%)
  between operations  13.6 us (8%)
  starting transfers between devices  10.6 us (6%)
    gather x1, local copies, waits for them, and re-layouts, reconstruct(): nearby = values[:, near_index]  56 us
    gather x1, local copies, waits for them, and re-layouts, shards(): atm_flux[:, cell_map[0]].reshape(fields, region_count, local_count, piece)  14.9 us
    reduce_max x1, other arithmetic, reconstruct(): upper = jnp.maximum(values, jnp.max(nearby, axis=1))  13.1 us
    all_to_all x1, blocking collectives, shards(): lax.all_to_all(leaving, 'region', split_axis=1, concat_axis=1, tiled=True)  11.9 us
    all_gather x1, waiting for transfers between devices, shards(): lax.all_gather(recon, 'local', axis=2, tiled=True)  8.7 us
    all_to_all x1, starting transfers between devices, shards(): lax.all_to_all(outgoing, 'region', split_axis=1, concat_axis=1, tiled=True)  7.28 us
    all_to_all x1, waiting for transfers between devices, shards(): lax.all_to_all(outgoing, 'region', split_axis=1, concat_axis=1, tiled=True)  7.08 us
    all_gather x1, blocking collectives, shards(): lax.all_gather(send_list, 'local', axis=0, tiled=True)  5.16 us
  transfers between devices with their start and end apart: 3, of which 3 were waited for; matrix products, arithmetic and copies ran while one was open for 0% of the time, Pallas kernels for 0%

commit v1 on v0

v1 whole, which is shorter than its diff:
```python
import functools

import jax
import jax.numpy as jnp
from jax import lax
from jax.experimental import pallas as pl
from jax.experimental.pallas import tpu as pltpu
from jax.sharding import PartitionSpec as P

ROWS = 16
HALF = 8
LANES = 128
DEPTH = 256
PER_ROW = DEPTH // LANES
STEP = 1024
WIDTH = 256
VMEM_LIMIT = 40 * 1024 * 1024


def lookup(table, index):
    row = lax.broadcasted_iota(jnp.int32, (DEPTH, WIDTH), 0).astype(jnp.bfloat16)
    results = []
    for at in range(0, index.shape[1], WIDTH):
        here = index[:, at : at + WIDTH]
        low = (here & (DEPTH - 1)).astype(jnp.bfloat16)
        hot = jnp.where(row == low, jnp.bfloat16(1), jnp.bfloat16(0))
        found = jnp.dot(table, hot, preferred_element_type=jnp.float32)
        high = jnp.broadcast_to(here // DEPTH, (ROWS, WIDTH))
        result = found[:ROWS]
        for part in range(1, table.shape[0] // ROWS):
            result = jnp.where(high == part, found[part * ROWS : (part + 1) * ROWS], result)
        results.append(result)
    return jnp.concatenate(results, axis=1)


def copies_of(sources, targets, sems, first=0):
    return [
        pltpu.make_async_copy(source, target, sems.at[first + at])
        for at, (source, target) in enumerate(zip(sources, targets))
    ]


def message_rows(fields, twins):
    return 2 * fields if twins == 2 else ROWS


def order_kernel(twins, map_hbm, flux_hbm, out_hbm, map_ref, flux_ref, out_ref, table, sems):
    fields, cells = flux_ref.shape
    steps = cells // STEP
    spans = [pl.ds(step * STEP, STEP) for step in range(steps)]
    needed = copies_of([flux_hbm.at[:, span] for span in spans], [flux_ref.at[:, span] for span in spans], sems)
    needed += copies_of((map_hbm,), (map_ref,), sems, 2 * steps)
    for copy in needed:
        copy.start()
    table[...] = jnp.zeros_like(table)
    for copy in needed:
        copy.wait()
    for part in range(cells // DEPTH):
        table[part * ROWS : part * ROWS + fields] = flux_ref[:, part * DEPTH : (part + 1) * DEPTH]
    rows = message_rows(fields, twins)
    written = []
    for step in range(steps):
        found = lookup(table[...], map_ref[:, step * STEP : (step + 1) * STEP])
        pieces = [found[:, at : at + LANES] for at in range(0, STEP, LANES)]
        if twins == 2:
            pieces = [
                jnp.concatenate([pieces[at][:fields], pieces[at ^ 2][:fields]], axis=0) for at in range(len(pieces))
            ]
        for at, piece in enumerate(pieces):
            first = (step * len(pieces) + at) * rows
            out_ref[first : first + rows] = piece.astype(jnp.bfloat16)
        span = pl.ds(step * len(pieces) * rows, len(pieces) * rows)
        written.append(pltpu.make_async_copy(out_ref.at[span], out_hbm.at[span], sems.at[steps + step]))
        written[-1].start()
    for copy in written:
        copy.wait()


def select_kernel(after_ref, list_hbm, near_hbm, x_hbm, y_hbm, *refs):
    selected, (list_ref, near_ref, x_ref, y_ref, sems) = refs[:-5], refs[-5:]
    copies = copies_of((list_hbm, near_hbm, x_hbm, y_hbm), (list_ref, near_ref, x_ref, y_ref), sems)
    for copy in copies:
        copy.start()
    for copy in copies:
        copy.wait()
    me = lax.axis_index("local")
    cap = list_ref.shape[2]
    count = list_ref.shape[1] // len(selected)
    near_count = near_ref.shape[0]
    for twin, stencil_ref in reversed(list(enumerate(selected))):
        for at in range(count * cap):
            block = list_ref[0, me ^ (2 * twin) ^ (at // cap), at % cap]
            columns = pl.ds(pl.multiple_of(block * LANES, LANES), LANES)
            stencil_ref[at, :near_count] = near_ref[:, columns].astype(jnp.float32)
            stencil_ref[at, near_count : 2 * near_count] = x_ref[:, columns]
            stencil_ref[at, 2 * near_count : 3 * near_count] = y_ref[:, columns]
            rest = (ROWS - 3 * near_count, LANES)
            stencil_ref[at, 3 * near_count :] = jnp.broadcast_to(block, rest).astype(jnp.float32)


def fetch_kernel(after_ref, map_hbm, *refs):
    count = (len(refs) - 3) // 2
    sources, moves_ref, targets, (map_ref, sems) = refs[:count], refs[count], refs[count + 1 : -2], refs[-2:]
    (needed,) = copies_of((map_hbm,), (map_ref,), sems, count)
    others = copies_of(sources, targets, sems)
    for copy in [needed] + others:
        copy.start()
    needed.wait()
    moves = lax.broadcasted_iota(jnp.int32, moves_ref.shape, 0) == map_ref[...]
    moves_ref[...] = jnp.where(moves, 1.0, 0.0).astype(jnp.bfloat16)
    for copy in others:
        copy.wait()


def rebuild(near_count, table, stencil, own, shift):
    near = stencil[:near_count].astype(jnp.int32)
    index = jnp.concatenate([near[j : j + 1] for j in range(near_count)], axis=1)
    found = lookup(table, index)
    upper = lower = own
    slope_x = slope_y = jnp.zeros_like(own)
    for j in range(near_count):
        value = found[:, j * LANES : (j + 1) * LANES]
        change = value - own
        slope_x += stencil[near_count + j : near_count + j + 1] * change
        slope_y += stencil[2 * near_count + j : 2 * near_count + j + 1] * change
        upper, lower = jnp.maximum(upper, value), jnp.minimum(lower, value)
    steep = jnp.abs(slope_x) + jnp.abs(slope_y)
    factor = jnp.minimum(1.0, (upper - lower) / jnp.maximum(steep, 1.0))
    results = [own, factor * slope_x, factor * slope_y]
    if shift:
        spare = jnp.zeros((shift, LANES), jnp.float32)
        results = [jnp.concatenate([result[shift:], spare], axis=0) for result in results]
    return results


def own_cells(near_count, table, stencil_ref):
    slots = stencil_ref.shape[0]
    tile = (ROWS, DEPTH)
    column = lax.broadcasted_iota(jnp.int32, tile, 1) - lax.broadcasted_iota(jnp.int32, tile, 0)
    blocks = [stencil_ref[at, 3 * near_count : 3 * near_count + 1].astype(jnp.int32) for at in range(slots)]
    picks = [
        jnp.where(jnp.concatenate([block // PER_ROW * ROWS] * PER_ROW, axis=1) == column, 1.0, 0.0) for block in blocks
    ]
    found = jnp.dot(
        jnp.concatenate(picks, axis=0).astype(jnp.bfloat16), table, preferred_element_type=jnp.float32
    )
    owns = []
    for at, block in enumerate(blocks):
        rows = found[at * ROWS : (at + 1) * ROWS]
        odd = jnp.broadcast_to(block % PER_ROW, (ROWS, LANES))
        owns.append(jnp.where(odd == 1, rows[:, LANES:], rows[:, :LANES]))
    return owns


def outer_kernel(twins, near_count, fields, after_ref, cells_ref, *refs):
    selected, refs = refs[:twins], refs[twins:]
    out_refs, (tables, owns) = refs[:-2], refs[-2:]
    cap = owns.shape[1]
    rows = message_rows(fields, twins)
    for twin in range(twins):
        for block in range(tables.shape[1] // ROWS * PER_ROW):
            part, column = block // PER_ROW, block % PER_ROW * LANES
            first = block * rows + HALF * twin
            tables[twin, part * ROWS : (part + 1) * ROWS, column : column + LANES] = cells_ref[first : first + ROWS]
    for twin, stencil_ref in enumerate(selected):
        for at, own in enumerate(own_cells(near_count, tables[twin], stencil_ref)):
            if at < cap:
                owns[twin, at] = own
                continue
            shift = twin * (fields - HALF)
            results = rebuild(near_count, tables[twin], stencil_ref[at], own, shift)
            for kind, result in enumerate(results):
                out_refs[at // cap - 1][twin, at % cap * len(results) + kind] = result.astype(jnp.bfloat16)


def inner_kernel(near_count, fields, tables, owns, *refs):
    selected, out_ref = refs[:-1], refs[-1]
    for twin, stencil_ref in enumerate(selected):
        for at in range(owns.shape[1]):
            own = owns[twin, at]
            shift = twin * (fields - HALF)
            results = rebuild(near_count, tables[twin], stencil_ref[at], own, shift)
            for kind, result in enumerate(results):
                out_ref[twin, at * len(results) + kind] = result.astype(jnp.bfloat16)


def remap_kernel(packed, fields, cover_ref, count_ref, weight_ref, moves_ref, *refs):
    received, (out_ref, source_ref) = refs[:-2], refs[-2:]
    me = lax.axis_index("local")
    ocean_blocks, slots, kinds = weight_ref.shape[:3]
    cap = source_ref.shape[1] // kinds
    for apart, piece_ref in enumerate(received):
        for twin in range(piece_ref.shape[0]):
            source_ref[me ^ apart ^ (2 * twin)] = piece_ref[twin]
    results = []
    for block in range(ocean_blocks):
        values, weights = [], []
        for slot in range(slots):
            at = cover_ref[block, slot]
            live = slot < count_ref[block]
            for kind in range(kinds):
                value = source_ref[at // cap, at % cap * kinds + kind]
                values.append(jnp.where(live, value, jnp.zeros_like(value)))
                weights.append(weight_ref[block, slot, kind])
        product = lax.dot_general(
            jnp.concatenate(values, axis=1),
            jnp.concatenate(weights, axis=1),
            (((1,), (1,)), ((), ())),
            preferred_element_type=jnp.float32,
        )
        results.append(product)
    remapped = jnp.concatenate(results, axis=1)
    cells = remapped.shape[1]
    coarse = remapped.astype(jnp.bfloat16)
    fine = (remapped - coarse.astype(jnp.float32)).astype(jnp.bfloat16)
    both = jnp.concatenate([coarse, fine], axis=0)
    moved = jnp.dot(both, moves_ref[...], preferred_element_type=jnp.float32)
    moved = moved[:ROWS] + moved[ROWS:]
    if not packed:
        out_ref[...] = moved[:fields]
        return
    half = fields // 2
    rows = out_ref.shape[1]
    listed = listing(out_ref.shape[0])
    side = lax.broadcasted_iota(jnp.int32, (rows, LANES), 1) < LANES // 2
    for pair in range(cells // LANES):
        columns = moved[:, pair * LANES : (pair + 1) * LANES]
        first, second = columns[:rows], columns[half : half + rows]
        out_ref[listed.index(2 * pair)] = jnp.where(side, first, pltpu.roll(second, LANES // 2, 1))
        out_ref[listed.index(2 * pair + 1)] = jnp.where(side, pltpu.roll(first, LANES // 2, 1), second)


def land_kernel(landed_ref, out_ref):
    count = landed_ref.shape[0]
    listed = listing(count)
    half = out_ref.shape[0] // 2
    side = lax.broadcasted_iota(jnp.int32, (half, LANES), 1) < LANES // 2
    for pair in range(count // 2):
        even, odd = landed_ref[listed.index(2 * pair), :half], landed_ref[listed.index(2 * pair + 1), :half]
        columns = pl.ds(pair * LANES, LANES)
        out_ref[:half, columns] = jnp.where(side, even, pltpu.roll(odd, LANES // 2, 1))
        out_ref[half:, columns] = jnp.where(side, pltpu.roll(even, LANES // 2, 1), odd)


def send(array, axis, apart):
    return lax.ppermute(array, axis, [(at, at ^ apart) for at in range(lax.axis_size(axis))])


def listing(count):
    return sorted(range(count), key=lambda at: (abs(2 * at - count + 1), -at))


def swap(pieces, axis):
    groups = [listing(lax.axis_size(axis))]
    pieces = pieces.transpose(1, 0, 2)
    swapped = lax.all_to_all(pieces, axis, split_axis=1, concat_axis=1, axis_index_groups=groups, tiled=True)
    return swapped.transpose(1, 0, 2)


SPACES = {"s": pltpu.SMEM, "v": pltpu.VMEM, "h": pltpu.HBM, "a": pl.ANY}


def call(kernel, outs, memories, scratch=(), out_memory="v", flops=0, moved=0):
    if isinstance(outs, list):
        out_specs = [pl.BlockSpec(memory_space=SPACES[kind]) for kind in (out_memory * len(outs))[: len(outs)]]
    else:
        out_specs = pl.BlockSpec(memory_space=SPACES[out_memory])
    return pl.pallas_call(
        kernel,
        out_shape=outs,
        in_specs=[pl.BlockSpec(memory_space=SPACES[kind]) for kind in memories],
        out_specs=out_specs,
        scratch_shapes=list(scratch),
        cost_estimate=pl.CostEstimate(flops=flops, bytes_accessed=moved, transcendentals=0),
        compiler_params=pltpu.CompilerParams(vmem_limit_bytes=VMEM_LIMIT),
    )


def shards(
    atm_flux,
    cell_map,
    neighbours,
    coef_x,
    coef_y,
    send_list,
    cover,
    cover_count,
    weights,
    ocean_map,
):
    fields, cells = atm_flux.shape
    region_count = lax.axis_size("region")
    local_count = lax.axis_size("local")
    everyone = ("region", "local")
    devices = region_count * local_count
    piece = cells // devices
    blocks = cells // LANES
    table = (cells // DEPTH * ROWS, DEPTH)
    shaped = jax.ShapeDtypeStruct
    twins = 2 if local_count == 4 and piece == LANES else 1
    cap = send_list.shape[2]
    aparts = local_count // twins
    near_count = neighbours.shape[0]
    kinds = weights.shape[2]
    ocean_cells = ocean_map.shape[1]

    def stay(*arrays):
        return [pltpu.with_memory_space_constraint(array, pltpu.HBM) for array in arrays]

    def scratch(array):
        return pltpu.VMEM(array.shape, array.dtype)

    rows = message_rows(fields, twins)
    messages = (blocks * rows, LANES)
    ordered = call(
        functools.partial(order_kernel, twins),
        shaped(messages, jnp.bfloat16),
        "hh",
        [
            scratch(cell_map),
            scratch(atm_flux),
            pltpu.VMEM(messages, jnp.bfloat16),
            pltpu.VMEM(table, jnp.bfloat16),
            pltpu.SemaphoreType.DMA((2 * (cells // STEP) + 1,)),
        ],
        out_memory="h",
    )(*stay(cell_map, atm_flux))

    stencil = shaped((aparts * cap, ROWS, LANES), jnp.float32)
    selected = call(
        select_kernel,
        [stencil] * twins,
        "ahhhh",
        [
            pltpu.SMEM(send_list.shape, send_list.dtype),
            scratch(neighbours),
            scratch(coef_x),
            scratch(coef_y),
            pltpu.SemaphoreType.DMA((4,)),
        ],
        moved=3_000_000,
    )(ordered, *stay(send_list, neighbours, coef_x, coef_y))
    selected = [selected[0]] + [send(array, "local", 2) for array in selected[1:]]

    later = [cover, cover_count, weights]
    moves, cover, cover_count, weights = call(
        fetch_kernel,
        [
            shaped((ocean_cells, ocean_cells), jnp.bfloat16),
            pltpu.SMEM(cover.shape, cover.dtype),
            pltpu.SMEM(cover_count.shape, cover_count.dtype),
            shaped(weights.shape, weights.dtype),
        ],
        "ah" + "h" * len(later),
        [scratch(ocean_map), pltpu.SemaphoreType.DMA((len(later) + 1,))],
        out_memory="vssv",
        moved=3_000_000,
    )(ordered, *stay(ocean_map, *later))

    if piece == LANES:
        coupled = lax.all_to_all(ordered, everyone, split_axis=0, concat_axis=0, tiled=True)
    else:
        outgoing = ordered.reshape(blocks, rows, LANES)[:, :fields].transpose(1, 0, 2).reshape(fields, devices, piece)
        coupled = lax.all_to_all(outgoing, everyone, split_axis=1, concat_axis=1, tiled=True)
        coupled = coupled.reshape(fields, blocks, LANES).transpose(1, 0, 2)
        coupled = jnp.pad(coupled, ((0, 0), (0, rows - fields), (0, 0))).reshape(messages)

    sent = shaped((twins, cap * kinds, ROWS, LANES), jnp.bfloat16)
    tables = shaped((twins,) + table, jnp.bfloat16)
    owns = shaped((twins, cap, ROWS, LANES), jnp.float32)
    work = 2 * twins * cap * table[0] * DEPTH * near_count * LANES
    *outer, tables, owns = call(
        functools.partial(outer_kernel, twins, near_count, fields),
        [sent] * (aparts - 1) + [tables, owns],
        "av" + "v" * twins,
        flops=work * (aparts - 1),
    )(moves, coupled, *selected)
    source = [send(array, "local", 1 + at) for at, array in enumerate(outer)]
    inner = call(
        functools.partial(inner_kernel, near_count, fields),
        sent,
        "vv" + "v" * twins,
        flops=work,
        moved=4_000_000,
    )(tables, owns, *selected)
    source = [inner] + source

    share = ocean_cells // region_count
    packed = share * 2 == LANES
    out_shape = (region_count, ROWS // 2, LANES) if packed else (fields, ocean_cells)
    leaving = call(
        functools.partial(remap_kernel, packed, fields),
        shaped(out_shape, jnp.float32),
        "ssvv" + "v" * aparts,
        [pltpu.VMEM((local_count, cap * kinds, ROWS, LANES), jnp.bfloat16)],
    )(cover, cover_count, weights, moves, *source)
    if packed:
        landed = swap(leaving, "region")
        return call(land_kernel, shaped((fields, ocean_cells), jnp.float32), "v")(landed)
    leaving = leaving.reshape(fields, region_count, share)
    landed = lax.all_to_all(leaving, "region", split_axis=1, concat_axis=1, tiled=True)
    return landed.reshape(fields, ocean_cells)


def solution(mesh):
    return jax.shard_map(
        shards,
        mesh=mesh,
        in_specs=(
            P(None, ("region", "local")),
            P(("region", "local"), None),
            P(None, ("region", "local")),
            P(None, ("region", "local")),
            P(None, ("region", "local")),
            P(("region", "local"), None, None),
            P(("region", "local"), None),
            P(("region", "local")),
            P(("region", "local"), None, None, None, None),
            P(("region", "local"), None),
        ),
        out_specs=P(None, ("region", "local")),
        check_vma=False,
    )
```

time: 171 us -> 31.1 us (0.18)
  local copies, waits for them, and re-layouts: 92.6 us -> 0 us
  other arithmetic: 15.5 us -> 0 us
  waiting for transfers between devices: 20 us -> 4.8 us
  between operations: 13.6 us -> 0.04 us
  blocking collectives: 17.1 us -> 8.45 us
  Pallas kernels: 0 us -> 7.61 us
    gather x6 -> x0, local copies, waits for them, and re-layouts: 73.2 us -> none  [the longest x1 56 us: reconstruct(): nearby = values[:, near_index]]
    reduce_max x1 -> x0, other arithmetic: 13.1 us -> none  [reconstruct(): upper = jnp.maximum(values, jnp.max(nearby, axis=1))]
    all_to_all x2 -> x1, waiting for transfers between devices: 11.3 us -> 2.47 us  [shards(): lax.all_to_all(ordered, everyone, split_axis=0, concat_axis=0, tiled=True)]
    all_gather x1 -> x0, waiting for transfers between devices: 8.7 us -> none  [shards(): lax.all_gather(recon, 'local', axis=2, tiled=True)]
    pallas_call x0 -> x7, Pallas kernels: none -> 7.61 us  [the longest x1 2.23 us: shards(): call(functools.partial(order_kernel, twins), shaped(messages, jnp.bfloat1...]
    all_gather x1 -> x0, blocking collectives: 5.16 us -> none  [shards(): lax.all_gather(send_list, 'local', axis=0, tiled=True)]
    reduce_sum x2 -> x0, local copies, waits for them, and re-layouts: 4.48 us -> none  [the longest x1 2.25 us: reconstruct(): slope_y = jnp.sum(weight_y[None] * change, axis=1)]
    all_to_all x1, blocking collectives: 11.9 us -> 8.45 us  [swap(): lax.all_to_all(pieces, axis, split_axis=1, concat_axis=1, axis_index_grou...]
  transfers between devices with their start and end apart: 3 -> 3, of which waited for: 3 -> 3; matrix products, arithmetic and copies ran while one was open for 0% -> 0% of each run, Pallas kernels for 0% -> 10%
where the time goes in v1:
time: 31.1 us; the launch traced here: 30.7 us
  starting transfers between devices  9.79 us (31%)
  blocking collectives  8.45 us (27%)
  Pallas kernels  7.61 us (24%)
  waiting for transfers between devices  4.8 us (15%)
    all_to_all x1, blocking collectives, swap(): lax.all_to_all(pieces, axis, split_axis=1, concat_axis=1, axis_index_grou...  8.45 us
    all_to_all x1, starting transfers between devices, shards(): lax.all_to_all(ordered, everyone, split_axis=0, concat_axis=0, tiled=True)  7.3 us
    ppermute x2, starting transfers between devices, send(): lax.ppermute(array, axis, [(at, at ^ apart) for at in range(lax.axis_size...  2.49 us
    all_to_all x1, waiting for transfers between devices, shards(): lax.all_to_all(ordered, everyone, split_axis=0, concat_axis=0, tiled=True)  2.47 us
    ppermute x2, waiting for transfers between devices, send(): lax.ppermute(array, axis, [(at, at ^ apart) for at in range(lax.axis_size...  2.33 us
    pallas_call x1, Pallas kernels, shards(): call(functools.partial(order_kernel, twins), shaped(messages, jnp.bfloat1...  2.23 us
    pallas_call x1, Pallas kernels, shards(): call(fetch_kernel, [shaped((ocean_cells, ocean_cells), jnp.bfloat16), plt...  1.46 us
    pallas_call x1, Pallas kernels, shards(): call(select_kernel, [stencil] * twins, 'ahhhh', [pltpu.SMEM(send_list.sha...  0.98 us
  transfers between devices with their start and end apart: 3, of which 3 were waited for; matrix products, arithmetic and copies ran while one was open for 0% of the time, Pallas kernels for 10%

profile of v1, /device:TPU:0, one launch (start us, length us, event | category | flops | bytes accessed | tf_op | source)
XLA Modules:
  0.0 30.7 jit_solution(16641772940893196450)
XLA Ops:
  0.0 2.2 %shard_map.100.after_ref = bf16[768,128]{1,0:T(8,128)(2,1)} custom-call(s32[1,4096]{1,0:T(1,128)} %map_hbm.2, bf16[12,4096]{1,0:T(8,128)(2,1)} %flux_hbm.1), custom_call_target="tpu_custom_call" | custom-call | tf_op jit(solution)/shard_map/pallas_call | solution.py:315
  2.2 7.3 %all-to-all-start = ((bf16[32,24,128]{2,1,0:T(8,128)(2,1)}), bf16[32,24,128]{2,1,0:T(8,128)(2,1)S(1)}, u32[]{:S(2)}, u32[]{:S(2)}) async-start(bf16[32,24,128]{2,1,0:T(8,128)(2,1)} %bitcast), calls=%async_computation | async-start | bytes 393216 | tf_op jit(solution)/shard_map/all_to_all | solution.py:361
  9.5 1.0 %shard_map.102 = (f32[8,16,128]{2,1,0:T(8,128)S(1)}, f32[8,16,128]{2,1,0:T(8,128)S(1)}) custom-call(bf16[768,128]{1,0:T(8,128)(2,1)} %shard_map.100.after_ref, s32[1,4,4]{2,1,0:T(4,128)} %list_hbm.1, s32[4,4096]{1,0:T(4,128)} %near_hbm.1, f32[4,4096]{1,0:T(4,128)} %x_hbm.1, f32[4,4096]{1,0:T(4,128)} %y_hbm.1), custom_call_target="tpu_custom_call" | custom-call | bytes 3000000 | tf_op jit(solution)/shard_map/pallas_call | solution.py:330
  10.5 1.8 %collective-permute-start = (f32[8,16,128]{2,1,0:T(8,128)S(1)}, f32[8,16,128]{2,1,0:T(8,128)S(1)}, u32[]{:S(2)}, u32[]{:S(2)}) collective-permute-start(f32[8,16,128]{2,1,0:T(8,128)S(1)} %get-tuple-element.19), channel_id=1, source_target_pairs={{0,2},{1,3},{2,0},{3,1},{4,6},{5,7},{6,4},{7,5},{8,10},{9,11},{10,... | collective-permute-start | bytes 196616 | tf_op jit(solution)/shard_map/ppermute | solution.py:246
  12.4 1.5 %shard_map.101 = (bf16[512,512]{1,0:T(8,128)(2,1)S(1)}, s32[4,4]{1,0:T(4,128)S(4)}, s32[4]{0:T(128)S(4)}, bf16[4,4,3,128,128]{4,3,2,1,0:T(8,128)(2,1)S(1)}) custom-call(bf16[768,128]{1,0:T(8,128)(2,1)} %shard_map.100.after_ref, s32[1,512]{1,0:T(1,128)} %map_hbm.3, s32[4,4]{1,0:T(4,128)} %refs_0_.1, s32[4]{0:T(128)} %refs_1_.1, ...), custom_call_target="tpu_custom_call" | custom-call | bytes 3000000 | tf_op jit(solution)/shard_map/pallas_call | solution.py:346
  13.8 2.1 %collective-permute-done.refs_1_ = f32[8,16,128]{2,1,0:T(8,128)S(1)} collective-permute-done((f32[8,16,128]{2,1,0:T(8,128)S(1)}, f32[8,16,128]{2,1,0:T(8,128)S(1)}, u32[]{:S(2)}, u32[]{:S(2)}) %collective-permute-start) | collective-permute-done | bytes 65568 | tf_op jit(solution)/shard_map/ppermute | solution.py:246
  16.0 2.5 %all-to-all-done = bf16[32,24,128]{2,1,0:T(8,128)(2,1)S(1)} async-done(((bf16[32,24,128]{2,1,0:T(8,128)(2,1)}), bf16[32,24,128]{2,1,0:T(8,128)(2,1)S(1)}, u32[]{:S(2)}, u32[]{:S(2)}) %all-to-all-start) | async-done | bytes 196640 | tf_op jit(solution)/shard_map/all_to_all | solution.py:361
  18.4 0.8 %shard_map.103 = (bf16[2,12,16,128]{3,2,1,0:T(8,128)(2,1)S(1)}, bf16[2,256,256]{2,1,0:T(8,128)(2,1)S(1)}, f32[2,4,16,128]{3,2,1,0:T(8,128)S(1)}) custom-call(bf16[512,512]{1,0:T(8,128)(2,1)S(1)} %get-tuple-element.17.after_ref.moves_ref, bf16[768,128]{1,0:T(8,128)(2,1)S(1)} %bitcast.4, f32[8,16,128]{2,1,0:T(8,128)S(1)} %get-tuple-element.18.refs_0_, ...), custom_call_target="tpu_custom_call" | custom-call | flops 536870912 | tf_op jit(solution)/shard_map/pallas_call | solution.py:372
  19.2 0.7 %collective-permute-start.1 = (bf16[2,12,16,128]{3,2,1,0:T(8,128)(2,1)S(1)}, bf16[2,12,16,128]{3,2,1,0:T(8,128)(2,1)S(1)}, u32[]{:S(2)}, u32[]{:S(2)}) collective-permute-start(bf16[2,12,16,128]{3,2,1,0:T(8,128)(2,1)S(1)} %get-tuple-element.22), channel_id=1, source_target_pairs={{0,1},{1,0},{2,3},{3,2},{4,5},{5,4},{6,7},{7,6},{8,9},{9,8},{10,11... | collective-permute-start | bytes 294920 | tf_op jit(solution)/shard_map/ppermute | solution.py:246
  19.9 0.7 %shard_map.104.refs_0_ = bf16[2,12,16,128]{3,2,1,0:T(8,128)(2,1)S(1)} custom-call(bf16[2,256,256]{2,1,0:T(8,128)(2,1)S(1)} %get-tuple-element.20.tables, f32[2,4,16,128]{3,2,1,0:T(8,128)S(1)} %get-tuple-element.21.owns, f32[8,16,128]{2,1,0:T(8,128)S(1)} %get-tuple-element.18.refs_0_, f32[8,16,128]{2,1,0:T(8,128)S(1)} %collective-permute-done.refs_1_), custom_call_target="tpu_custom_call" | custom-call | flops 536870912 | bytes 4000000 | tf_op jit(solution)/shard_map/pallas_call | solution.py:379
  20.6 0.2 collective-permute-done.1.refs_1_
  20.8 0.7 %shard_map.105 = f32[8,8,128]{2,1,0:T(8,128)S(1)} custom-call(s32[4,4]{1,0:T(4,128)S(4)} %get-tuple-element.14.cover_ref, s32[4]{0:T(128)S(4)} %get-tuple-element.15.count_ref, bf16[4,4,3,128,128]{4,3,2,1,0:T(8,128)(2,1)S(1)} %get-tuple-element.16.weight_ref, bf16[512,512]{1,0:T(8,128)(2,1)S(1)} %get-tuple-element.17.after_ref.moves_ref, ...), custom_call_target="tpu_custom_call" | custom-call | tf_op jit(solution)/shard_map/pallas_call | solution.py:391
  21.6 8.5 %all_to_all.16 = f32[8,8,128]{2,0,1:T(8,128)S(1)} all-to-all(f32[8,8,128]{2,0,1:T(8,128)S(1)} %bitcast.5), channel_id=1, replica_groups={{16,12,20,8,24,4,28,0},{17,13,21,9,25,5,29,1},{18,14,22,10,26,6,30,2},{..., dimensions={1} | all-to-all | bytes 65536 | tf_op jit(solution)/shard_map/all_to_all | solution.py:256
  30.0 0.7 %shard_map.106 = f32[12,512]{1,0:T(8,128)} custom-call(f32[8,8,128]{2,1,0:T(8,128)S(1)} %bitcast.6), custom_call_target="tpu_custom_call" | custom-call | tf_op jit(solution)/shard_map/pallas_call | solution.py:399
Async XLA Ops:
  2.2 16.2 %all-to-all-start = ((bf16[32,24,128]{2,1,0:T(8,128)(2,1)}), bf16[32,24,128]{2,1,0:T(8,128)(2,1)S(1)}, u32[]{:S(2)}, u32[]{:S(2)}) async-start(bf16[32,24,128]{2,1,0:T(8,128)(2,1)} %bitcast), calls=%async_computation | async-start | bytes 393216 | tf_op jit(solution)/shard_map/all_to_all | solution.py:361
  10.5 5.4 %collective-permute-start = (f32[8,16,128]{2,1,0:T(8,128)S(1)}, f32[8,16,128]{2,1,0:T(8,128)S(1)}, u32[]{:S(2)}, u32[]{:S(2)}) collective-permute-start(f32[8,16,128]{2,1,0:T(8,128)S(1)} %get-tuple-element.19), channel_id=1, source_target_pairs={{0,2},{1,3},{2,0},{3,1},{4,6},{5,7},{6,4},{7,5},{8,10},{9,11},{10,... | collective-permute-start | bytes 196616 | tf_op jit(solution)/shard_map/ppermute | solution.py:246
  19.2 1.6 %collective-permute-start.1 = (bf16[2,12,16,128]{3,2,1,0:T(8,128)(2,1)S(1)}, bf16[2,12,16,128]{3,2,1,0:T(8,128)(2,1)S(1)}, u32[]{:S(2)}, u32[]{:S(2)}) collective-permute-start(bf16[2,12,16,128]{3,2,1,0:T(8,128)(2,1)S(1)} %get-tuple-element.22), channel_id=1, source_target_pairs={{0,1},{1,0},{2,3},{3,2},{4,5},{5,4},{6,7},{7,6},{8,9},{9,8},{10,11... | collective-permute-start | bytes 294920 | tf_op jit(solution)/shard_map/ppermute | solution.py:246

commit v2 on v1

--- a/solution.py
+++ b/solution.py
@@ -12,24 +12,44 @@
 LANES = 128
 DEPTH = 256
 PER_ROW = DEPTH // LANES
-STEP = 1024
+STEP = 512
 WIDTH = 256
 VMEM_LIMIT = 40 * 1024 * 1024
 
 
+def one_hot(index):
+    row = lax.broadcasted_iota(jnp.int32, (DEPTH, index.shape[1]), 0).astype(jnp.bfloat16)
+    low = (index & (DEPTH - 1)).astype(jnp.bfloat16)
+    return jnp.where(row == low, jnp.bfloat16(1), jnp.bfloat16(0))
+
+
+def choose(found, high, height):
+    high = jnp.broadcast_to(high, (height, found.shape[1]))
+    result = found[:height]
+    for part in range(1, found.shape[0] // height):
+        result = jnp.where(high == part, found[part * height : (part + 1) * height], result)
+    return result
+
+
 def lookup(table, index):
-    row = lax.broadcasted_iota(jnp.int32, (DEPTH, WIDTH), 0).astype(jnp.bfloat16)
     results = []
     for at in range(0, index.shape[1], WIDTH):
         here = index[:, at : at + WIDTH]
-        low = (here & (DEPTH - 1)).astype(jnp.bfloat16)
-        hot = jnp.where(row == low, jnp.bfloat16(1), jnp.bfloat16(0))
-        found = jnp.dot(table, hot, preferred_element_type=jnp.float32)
-        high = jnp.broadcast_to(here // DEPTH, (ROWS, WIDTH))
-        result = found[:ROWS]
-        for part in range(1, table.shape[0] // ROWS):
-            result = jnp.where(high == part, found[part * ROWS : (part + 1) * ROWS], result)
-        results.append(result)
+        found = jnp.dot(table, one_hot(here), preferred_element_type=jnp.float32)
+        results.append(choose(found, here // DEPTH, ROWS))
+    return jnp.concatenate(results, axis=1)
+
+
+def lookup_dense(table, index, parts):
+    results = []
+    for at in range(0, index.shape[1], WIDTH):
+        here = index[:, at : at + WIDTH]
+        found = jnp.dot(table, one_hot(here), preferred_element_type=jnp.float32)
+        high = here // DEPTH
+        upper = choose(found[: HALF * parts], high, HALF)
+        lower = choose(found[HALF * parts :], high // 2, HALF)
+        odd = jnp.broadcast_to(high % 2, lower.shape)
+        results.append(jnp.concatenate([upper, jnp.where(odd == 1, pltpu.roll(lower, HALF // 2, 0), lower)], axis=0))
     return jnp.concatenate(results, axis=1)
 
 
@@ -47,20 +67,22 @@
 def order_kernel(twins, map_hbm, flux_hbm, out_hbm, map_ref, flux_ref, out_ref, table, sems):
     fields, cells = flux_ref.shape
     steps = cells // STEP
-    spans = [pl.ds(step * STEP, STEP) for step in range(steps)]
+    spans = [pl.ds(at, cells // 4) for at in range(0, cells, cells // 4)]
     needed = copies_of([flux_hbm.at[:, span] for span in spans], [flux_ref.at[:, span] for span in spans], sems)
-    needed += copies_of((map_hbm,), (map_ref,), sems, 2 * steps)
+    needed += copies_of((map_hbm,), (map_ref,), sems, 4)
     for copy in needed:
         copy.start()
-    table[...] = jnp.zeros_like(table)
     for copy in needed:
         copy.wait()
-    for part in range(cells // DEPTH):
-        table[part * ROWS : part * ROWS + fields] = flux_ref[:, part * DEPTH : (part + 1) * DEPTH]
+    parts, rest = cells // DEPTH, fields - HALF
+    for part in range(parts):
+        columns = slice(part * DEPTH, (part + 1) * DEPTH)
+        table[part * HALF : (part + 1) * HALF] = flux_ref[:HALF, columns]
+        table[parts * HALF + part * rest : parts * HALF + (part + 1) * rest] = flux_ref[HALF:, columns]
     rows = message_rows(fields, twins)
     written = []
     for step in range(steps):
-        found = lookup(table[...], map_ref[:, step * STEP : (step + 1) * STEP])
+        found = lookup_dense(table[...], map_ref[:, step * STEP : (step + 1) * STEP], parts)
         pieces = [found[:, at : at + LANES] for at in range(0, STEP, LANES)]
         if twins == 2:
             pieces = [
@@ -70,7 +92,7 @@
             first = (step * len(pieces) + at) * rows
             out_ref[first : first + rows] = piece.astype(jnp.bfloat16)
         span = pl.ds(step * len(pieces) * rows, len(pieces) * rows)
-        written.append(pltpu.make_async_copy(out_ref.at[span], out_hbm.at[span], sems.at[steps + step]))
+        written.append(pltpu.make_async_copy(out_ref.at[span], out_hbm.at[span], sems.at[5 + step]))
         written[-1].start()
     for copy in written:
         copy.wait()
@@ -99,15 +121,15 @@
 
 
 def fetch_kernel(after_ref, map_hbm, *refs):
-    count = (len(refs) - 3) // 2
-    sources, moves_ref, targets, (map_ref, sems) = refs[:count], refs[count], refs[count + 1 : -2], refs[-2:]
+    count = (len(refs) - 4) // 2
+    sources, (moves_ref, high_ref), targets, (map_ref, sems) = refs[:count], refs[count : count + 2], refs[count + 2 : -2], refs[-2:]
     (needed,) = copies_of((map_hbm,), (map_ref,), sems, count)
     others = copies_of(sources, targets, sems)
     for copy in [needed] + others:
         copy.start()
     needed.wait()
-    moves = lax.broadcasted_iota(jnp.int32, moves_ref.shape, 0) == map_ref[...]
-    moves_ref[...] = jnp.where(moves, 1.0, 0.0).astype(jnp.bfloat16)
+    moves_ref[...] = one_hot(map_ref[...])
+    high_ref[...] = map_ref[...] // DEPTH
     for copy in others:
         copy.wait()
 
@@ -184,7 +206,7 @@
                 out_ref[twin, at * len(results) + kind] = result.astype(jnp.bfloat16)
 
 
-def remap_kernel(packed, fields, cover_ref, count_ref, weight_ref, moves_ref, *refs):
+def remap_kernel(packed, fields, cover_ref, count_ref, weight_ref, moves_ref, high_ref, *refs):
     received, (out_ref, source_ref) = refs[:-2], refs[-2:]
     me = lax.axis_index("local")
     ocean_blocks, slots, kinds = weight_ref.shape[:3]
@@ -213,8 +235,9 @@
     cells = remapped.shape[1]
     coarse = remapped.astype(jnp.bfloat16)
     fine = (remapped - coarse.astype(jnp.float32)).astype(jnp.bfloat16)
-    both = jnp.concatenate([coarse, fine], axis=0)
-    moved = jnp.dot(both, moves_ref[...], preferred_element_type=jnp.float32)
+    table = [part[:, at : at + DEPTH] for at in range(0, cells, DEPTH) for part in (coarse, fine)]
+    moved = jnp.dot(jnp.concatenate(table, axis=0), moves_ref[...], preferred_element_type=jnp.float32)
+    moved = choose(moved, high_ref[...], 2 * ROWS)
     moved = moved[:ROWS] + moved[ROWS:]
     if not packed:
         out_ref[...] = moved[:fields]
@@ -320,8 +343,8 @@
             scratch(cell_map),
             scratch(atm_flux),
             pltpu.VMEM(messages, jnp.bfloat16),
-            pltpu.VMEM(table, jnp.bfloat16),
-            pltpu.SemaphoreType.DMA((2 * (cells // STEP) + 1,)),
+            pltpu.VMEM((cells // DEPTH * fields, DEPTH), jnp.bfloat16),
+            pltpu.SemaphoreType.DMA((cells // STEP + 5,)),
         ],
         out_memory="h",
     )(*stay(cell_map, atm_flux))
@@ -343,17 +366,18 @@
     selected = [selected[0]] + [send(array, "local", 2) for array in selected[1:]]
 
     later = [cover, cover_count, weights]
-    moves, cover, cover_count, weights = call(
+    moves, high, cover, cover_count, weights = call(
         fetch_kernel,
         [
-            shaped((ocean_cells, ocean_cells), jnp.bfloat16),
+            shaped((DEPTH, ocean_cells), jnp.bfloat16),
+            shaped(ocean_map.shape, ocean_map.dtype),
             pltpu.SMEM(cover.shape, cover.dtype),
             pltpu.SMEM(cover_count.shape, cover_count.dtype),
             shaped(weights.shape, weights.dtype),
         ],
         "ah" + "h" * len(later),
         [scratch(ocean_map), pltpu.SemaphoreType.DMA((len(later) + 1,))],
-        out_memory="vssv",
+        out_memory="vvssv",
         moved=3_000_000,
     )(ordered, *stay(ocean_map, *later))
 
@@ -391,9 +415,9 @@
     leaving = call(
         functools.partial(remap_kernel, packed, fields),
         shaped(out_shape, jnp.float32),
-        "ssvv" + "v" * aparts,
+        "ssvvv" + "v" * aparts,
         [pltpu.VMEM((local_count, cap * kinds, ROWS, LANES), jnp.bfloat16)],
-    )(cover, cover_count, weights, moves, *source)
+    )(cover, cover_count, weights, moves, high, *source)
     if packed:
         landed = swap(leaving, "region")
         return call(land_kernel, shaped((fields, ocean_cells), jnp.float32), "v")(landed)

time: 31.1 us -> 31 us (level)
  no operation moved by 1% of the time
where the time goes in v2:
time: 31 us; the launch traced here: 30.6 us
  starting transfers between devices  9.79 us (32%)
  blocking collectives  8.45 us (27%)
  Pallas kernels  7.54 us (24%)
  waiting for transfers between devices  4.8 us (15%)
    all_to_all x1, blocking collectives, swap(): lax.all_to_all(pieces, axis, split_axis=1, concat_axis=1, axis_index_grou...  8.45 us
    all_to_all x1, starting transfers between devices, shards(): lax.all_to_all(ordered, everyone, split_axis=0, concat_axis=0, tiled=True)  7.3 us
    ppermute x2, starting transfers between devices, send(): lax.ppermute(array, axis, [(at, at ^ apart) for at in range(lax.axis_size...  2.49 us
    all_to_all x1, waiting for transfers between devices, shards(): lax.all_to_all(ordered, everyone, split_axis=0, concat_axis=0, tiled=True)  2.47 us
    ppermute x2, waiting for transfers between devices, send(): lax.ppermute(array, axis, [(at, at ^ apart) for at in range(lax.axis_size...  2.33 us
    pallas_call x1, Pallas kernels, shards(): call(functools.partial(order_kernel, twins), shaped(messages, jnp.bfloat1...  2.15 us
    pallas_call x1, Pallas kernels, shards(): call(fetch_kernel, [shaped((DEPTH, ocean_cells), jnp.bfloat16), shaped(oc...  1.46 us
    pallas_call x1, Pallas kernels, shards(): call(select_kernel, [stencil] * twins, 'ahhhh', [pltpu.SMEM(send_list.sha...  0.98 us
  transfers between devices with their start and end apart: 3, of which 3 were waited for; matrix products, arithmetic and copies ran while one was open for 0% of the time, Pallas kernels for 10%

profile of v2, /device:TPU:0, one launch (start us, length us, event | category | flops | bytes accessed | tf_op | source)
XLA Modules:
  0.0 30.6 jit_solution(14427660450543139512)
XLA Ops:
  0.0 2.1 %shard_map.100.after_ref = bf16[768,128]{1,0:T(8,128)(2,1)} custom-call(s32[1,4096]{1,0:T(1,128)} %map_hbm.2, bf16[12,4096]{1,0:T(8,128)(2,1)} %flux_hbm.1), custom_call_target="tpu_custom_call" | custom-call | tf_op jit(solution)/shard_map/pallas_call | solution.py:338
  2.2 7.3 %all-to-all-start = ((bf16[32,24,128]{2,1,0:T(8,128)(2,1)}), bf16[32,24,128]{2,1,0:T(8,128)(2,1)S(1)}, u32[]{:S(2)}, u32[]{:S(2)}) async-start(bf16[32,24,128]{2,1,0:T(8,128)(2,1)} %bitcast), calls=%async_computation | async-start | bytes 393216 | tf_op jit(solution)/shard_map/all_to_all | solution.py:385
  9.5 1.0 %shard_map.102 = (f32[8,16,128]{2,1,0:T(8,128)S(1)}, f32[8,16,128]{2,1,0:T(8,128)S(1)}) custom-call(bf16[768,128]{1,0:T(8,128)(2,1)} %shard_map.100.after_ref, s32[1,4,4]{2,1,0:T(4,128)} %list_hbm.1, s32[4,4096]{1,0:T(4,128)} %near_hbm.1, f32[4,4096]{1,0:T(4,128)} %x_hbm.1, f32[4,4096]{1,0:T(4,128)} %y_hbm.1), custom_call_target="tpu_custom_call" | custom-call | bytes 3000000 | tf_op jit(solution)/shard_map/pallas_call | solution.py:353
  10.4 1.8 %collective-permute-start = (f32[8,16,128]{2,1,0:T(8,128)S(1)}, f32[8,16,128]{2,1,0:T(8,128)S(1)}, u32[]{:S(2)}, u32[]{:S(2)}) collective-permute-start(f32[8,16,128]{2,1,0:T(8,128)S(1)} %get-tuple-element.21), channel_id=1, source_target_pairs={{0,2},{1,3},{2,0},{3,1},{4,6},{5,7},{6,4},{7,5},{8,10},{9,11},{10,... | collective-permute-start | bytes 196616 | tf_op jit(solution)/shard_map/ppermute | solution.py:269
  12.3 1.5 %shard_map.101 = (bf16[256,512]{1,0:T(8,128)(2,1)S(1)}, s32[1,512]{1,0:T(1,128)S(1)}, s32[4,4]{1,0:T(4,128)S(4)}, s32[4]{0:T(128)S(4)}, bf16[4,4,3,128,128]{4,3,2,1,0:T(8,128)(2,1)S(1)}) custom-call(bf16[768,128]{1,0:T(8,128)(2,1)} %shard_map.100.after_ref, s32[1,512]{1,0:T(1,128)} %map_hbm.3, s32[4,4]{1,0:T(4,128)} %refs_0_.1, s32[4]{0:T(128)} %refs_1_.1, ...), custom_call_target="tpu_custom_call" | custom-call | bytes 3000000 | tf_op jit(solution)/shard_map/pallas_call | solution.py:369
  13.7 2.1 %collective-permute-done.refs_1_ = f32[8,16,128]{2,1,0:T(8,128)S(1)} collective-permute-done((f32[8,16,128]{2,1,0:T(8,128)S(1)}, f32[8,16,128]{2,1,0:T(8,128)S(1)}, u32[]{:S(2)}, u32[]{:S(2)}) %collective-permute-start) | collective-permute-done | bytes 65568 | tf_op jit(solution)/shard_map/ppermute | solution.py:269
  15.9 2.5 %all-to-all-done = bf16[32,24,128]{2,1,0:T(8,128)(2,1)S(1)} async-done(((bf16[32,24,128]{2,1,0:T(8,128)(2,1)}), bf16[32,24,128]{2,1,0:T(8,128)(2,1)S(1)}, u32[]{:S(2)}, u32[]{:S(2)}) %all-to-all-start) | async-done | bytes 196640 | tf_op jit(solution)/shard_map/all_to_all | solution.py:385
  18.3 0.8 %shard_map.103 = (bf16[2,12,16,128]{3,2,1,0:T(8,128)(2,1)S(1)}, bf16[2,256,256]{2,1,0:T(8,128)(2,1)S(1)}, f32[2,4,16,128]{3,2,1,0:T(8,128)S(1)}) custom-call(bf16[256,512]{1,0:T(8,128)(2,1)S(1)} %get-tuple-element.18.after_ref.moves_ref, bf16[768,128]{1,0:T(8,128)(2,1)S(1)} %bitcast.4, f32[8,16,128]{2,1,0:T(8,128)S(1)} %get-tuple-element.20.refs_0_, ...), custom_call_target="tpu_custom_call" | custom-call | flops 536870912 | tf_op jit(solution)/shard_map/pallas_call | solution.py:396
  19.2 0.7 %collective-permute-start.1 = (bf16[2,12,16,128]{3,2,1,0:T(8,128)(2,1)S(1)}, bf16[2,12,16,128]{3,2,1,0:T(8,128)(2,1)S(1)}, u32[]{:S(2)}, u32[]{:S(2)}) collective-permute-start(bf16[2,12,16,128]{3,2,1,0:T(8,128)(2,1)S(1)} %get-tuple-element.24), channel_id=1, source_target_pairs={{0,1},{1,0},{2,3},{3,2},{4,5},{5,4},{6,7},{7,6},{8,9},{9,8},{10,11... | collective-permute-start | bytes 294920 | tf_op jit(solution)/shard_map/ppermute | solution.py:269
  19.8 0.7 %shard_map.104.refs_0_ = bf16[2,12,16,128]{3,2,1,0:T(8,128)(2,1)S(1)} custom-call(bf16[2,256,256]{2,1,0:T(8,128)(2,1)S(1)} %get-tuple-element.22.tables, f32[2,4,16,128]{3,2,1,0:T(8,128)S(1)} %get-tuple-element.23.owns, f32[8,16,128]{2,1,0:T(8,128)S(1)} %get-tuple-element.20.refs_0_, f32[8,16,128]{2,1,0:T(8,128)S(1)} %collective-permute-done.refs_1_), custom_call_target="tpu_custom_call" | custom-call | flops 536870912 | bytes 4000000 | tf_op jit(solution)/shard_map/pallas_call | solution.py:403
  20.6 0.2 collective-permute-done.1.refs_1_
  20.8 0.7 %shard_map.105 = f32[8,8,128]{2,1,0:T(8,128)S(1)} custom-call(s32[4,4]{1,0:T(4,128)S(4)} %get-tuple-element.15.cover_ref, s32[4]{0:T(128)S(4)} %get-tuple-element.16.count_ref, bf16[4,4,3,128,128]{4,3,2,1,0:T(8,128)(2,1)S(1)} %get-tuple-element.17.weight_ref, bf16[256,512]{1,0:T(8,128)(2,1)S(1)} %get-tuple-element.18.after_ref.moves_ref, ...), custom_call_target="tpu_custom_call" | custom-call | tf_op jit(solution)/shard_map/pallas_call | solution.py:415
  21.5 8.4 %all_to_all.16 = f32[8,8,128]{2,0,1:T(8,128)S(1)} all-to-all(f32[8,8,128]{2,0,1:T(8,128)S(1)} %bitcast.5), channel_id=1, replica_groups={{16,12,20,8,24,4,28,0},{17,13,21,9,25,5,29,1},{18,14,22,10,26,6,30,2},{..., dimensions={1} | all-to-all | bytes 65536 | tf_op jit(solution)/shard_map/all_to_all | solution.py:279
  29.9 0.7 %shard_map.106 = f32[12,512]{1,0:T(8,128)} custom-call(f32[8,8,128]{2,1,0:T(8,128)S(1)} %bitcast.6), custom_call_target="tpu_custom_call" | custom-call | tf_op jit(solution)/shard_map/pallas_call | solution.py:423
Async XLA Ops:
  2.2 16.2 %all-to-all-start = ((bf16[32,24,128]{2,1,0:T(8,128)(2,1)}), bf16[32,24,128]{2,1,0:T(8,128)(2,1)S(1)}, u32[]{:S(2)}, u32[]{:S(2)}) async-start(bf16[32,24,128]{2,1,0:T(8,128)(2,1)} %bitcast), calls=%async_computation | async-start | bytes 393216 | tf_op jit(solution)/shard_map/all_to_all | solution.py:385
  10.4 5.4 %collective-permute-start = (f32[8,16,128]{2,1,0:T(8,128)S(1)}, f32[8,16,128]{2,1,0:T(8,128)S(1)}, u32[]{:S(2)}, u32[]{:S(2)}) collective-permute-start(f32[8,16,128]{2,1,0:T(8,128)S(1)} %get-tuple-element.21), channel_id=1, source_target_pairs={{0,2},{1,3},{2,0},{3,1},{4,6},{5,7},{6,4},{7,5},{8,10},{9,11},{10,... | collective-permute-start | bytes 196616 | tf_op jit(solution)/shard_map/ppermute | solution.py:269
  19.2 1.6 %collective-permute-start.1 = (bf16[2,12,16,128]{3,2,1,0:T(8,128)(2,1)S(1)}, bf16[2,12,16,128]{3,2,1,0:T(8,128)(2,1)S(1)}, u32[]{:S(2)}, u32[]{:S(2)}) collective-permute-start(bf16[2,12,16,128]{3,2,1,0:T(8,128)(2,1)S(1)} %get-tuple-element.24), channel_id=1, source_target_pairs={{0,1},{1,0},{2,3},{3,2},{4,5},{5,4},{6,7},{7,6},{8,9},{9,8},{10,11... | collective-permute-start | bytes 294920 | tf_op jit(solution)/shard_map/ppermute | solution.py:269

commit v3 on v2

--- a/solution.py
+++ b/solution.py
@@ -31,16 +31,7 @@
     return result
 
 
-def lookup(table, index):
-    results = []
-    for at in range(0, index.shape[1], WIDTH):
-        here = index[:, at : at + WIDTH]
-        found = jnp.dot(table, one_hot(here), preferred_element_type=jnp.float32)
-        results.append(choose(found, here // DEPTH, ROWS))
-    return jnp.concatenate(results, axis=1)
-
-
-def lookup_dense(table, index, parts):
+def lookup(table, index, parts):
     results = []
     for at in range(0, index.shape[1], WIDTH):
         here = index[:, at : at + WIDTH]
@@ -62,6 +53,12 @@
 
 def message_rows(fields, twins):
     return 2 * fields if twins == 2 else ROWS
+
+
+def joined(own, twin):
+    first = lax.broadcasted_iota(jnp.int32, (HALF, LANES), 0) < HALF // 2
+    middle = jnp.where(first, own[HALF:], pltpu.roll(twin[HALF:], HALF // 2, 0))
+    return jnp.concatenate([own[:HALF], middle, twin[:HALF]], axis=0)
 
 
 def order_kernel(twins, map_hbm, flux_hbm, out_hbm, map_ref, flux_ref, out_ref, table, sems):
@@ -82,12 +79,10 @@
     rows = message_rows(fields, twins)
     written = []
     for step in range(steps):
-        found = lookup_dense(table[...], map_ref[:, step * STEP : (step + 1) * STEP], parts)
+        found = lookup(table[...], map_ref[:, step * STEP : (step + 1) * STEP], parts)
         pieces = [found[:, at : at + LANES] for at in range(0, STEP, LANES)]
         if twins == 2:
-            pieces = [
-                jnp.concatenate([pieces[at][:fields], pieces[at ^ 2][:fields]], axis=0) for at in range(len(pieces))
-            ]
+            pieces = [joined(pieces[at], pieces[at ^ 2]) for at in range(len(pieces))]
         for at, piece in enumerate(pieces):
             first = (step * len(pieces) + at) * rows
             out_ref[first : first + rows] = piece.astype(jnp.bfloat16)
@@ -134,10 +129,11 @@
         copy.wait()
 
 
-def rebuild(near_count, table, stencil, own, shift):
+def rebuild(near_count, table, stencil, own):
     near = stencil[:near_count].astype(jnp.int32)
     index = jnp.concatenate([near[j : j + 1] for j in range(near_count)], axis=1)
-    found = lookup(table, index)
+    parts = table.shape[0] // ROWS
+    found = lookup(table[: parts * (HALF + HALF // 2)], index, parts)
     upper = lower = own
     slope_x = slope_y = jnp.zeros_like(own)
     for j in range(near_count):
@@ -148,21 +144,21 @@
         upper, lower = jnp.maximum(upper, value), jnp.minimum(lower, value)
     steep = jnp.abs(slope_x) + jnp.abs(slope_y)
     factor = jnp.minimum(1.0, (upper - lower) / jnp.maximum(steep, 1.0))
-    results = [own, factor * slope_x, factor * slope_y]
-    if shift:
-        spare = jnp.zeros((shift, LANES), jnp.float32)
-        results = [jnp.concatenate([result[shift:], spare], axis=0) for result in results]
-    return results
+    return [own, factor * slope_x, factor * slope_y]
 
 
 def own_cells(near_count, table, stencil_ref):
     slots = stencil_ref.shape[0]
-    tile = (ROWS, DEPTH)
-    column = lax.broadcasted_iota(jnp.int32, tile, 1) - lax.broadcasted_iota(jnp.int32, tile, 0)
+    tile = (ROWS, table.shape[0])
+    row = lax.broadcasted_iota(jnp.int32, tile, 0)
+    upper = row < HALF
+    stride = jnp.where(upper, HALF, HALF // 2)
+    column = lax.broadcasted_iota(jnp.int32, tile, 1) - jnp.where(upper, row, HALF * (table.shape[0] // ROWS - 1) + row)
     blocks = [stencil_ref[at, 3 * near_count : 3 * near_count + 1].astype(jnp.int32) for at in range(slots)]
-    picks = [
-        jnp.where(jnp.concatenate([block // PER_ROW * ROWS] * PER_ROW, axis=1) == column, 1.0, 0.0) for block in blocks
-    ]
+    picks = []
+    for block in blocks:
+        part = jnp.concatenate([block // PER_ROW] * (table.shape[0] // LANES), axis=1)
+        picks.append(jnp.where(part * stride == column, 1.0, 0.0))
     found = jnp.dot(
         jnp.concatenate(picks, axis=0).astype(jnp.bfloat16), table, preferred_element_type=jnp.float32
     )
@@ -179,18 +175,21 @@
     out_refs, (tables, owns) = refs[:-2], refs[-2:]
     cap = owns.shape[1]
     rows = message_rows(fields, twins)
+    parts, rest = tables.shape[1] // ROWS, fields - HALF
     for twin in range(twins):
-        for block in range(tables.shape[1] // ROWS * PER_ROW):
-            part, column = block // PER_ROW, block % PER_ROW * LANES
-            first = block * rows + HALF * twin
-            tables[twin, part * ROWS : (part + 1) * ROWS, column : column + LANES] = cells_ref[first : first + ROWS]
+        tables[twin, parts * fields :] = jnp.zeros((parts * (ROWS - fields), DEPTH), jnp.bfloat16)
+        for block in range(parts * PER_ROW):
+            part, column = block // PER_ROW, slice(block % PER_ROW * LANES, (block % PER_ROW + 1) * LANES)
+            upper, lower = block * rows + twin * 2 * HALF, block * rows + HALF + twin * rest
+            tables[twin, part * HALF : (part + 1) * HALF, column] = cells_ref[upper : upper + HALF]
+            at = parts * HALF + part * rest
+            tables[twin, at : at + rest, column] = cells_ref[lower : lower + rest]
     for twin, stencil_ref in enumerate(selected):
         for at, own in enumerate(own_cells(near_count, tables[twin], stencil_ref)):
             if at < cap:
                 owns[twin, at] = own
                 continue
-            shift = twin * (fields - HALF)
-            results = rebuild(near_count, tables[twin], stencil_ref[at], own, shift)
+            results = rebuild(near_count, tables[twin], stencil_ref[at], own)
             for kind, result in enumerate(results):
                 out_refs[at // cap - 1][twin, at % cap * len(results) + kind] = result.astype(jnp.bfloat16)
 
@@ -200,8 +199,7 @@
     for twin, stencil_ref in enumerate(selected):
         for at in range(owns.shape[1]):
             own = owns[twin, at]
-            shift = twin * (fields - HALF)
-            results = rebuild(near_count, tables[twin], stencil_ref[at], own, shift)
+            results = rebuild(near_count, tables[twin], stencil_ref[at], own)
             for kind, result in enumerate(results):
                 out_ref[twin, at * len(results) + kind] = result.astype(jnp.bfloat16)
 
@@ -215,22 +213,27 @@
         for twin in range(piece_ref.shape[0]):
             source_ref[me ^ apart ^ (2 * twin)] = piece_ref[twin]
     results = []
-    for block in range(ocean_blocks):
+    for first in range(0, ocean_blocks, 2):
         values, weights = [], []
-        for slot in range(slots):
-            at = cover_ref[block, slot]
-            live = slot < count_ref[block]
-            for kind in range(kinds):
-                value = source_ref[at // cap, at % cap * kinds + kind]
-                values.append(jnp.where(live, value, jnp.zeros_like(value)))
-                weights.append(weight_ref[block, slot, kind])
+        for block in (first, first + 1):
+            tiles = []
+            for slot in range(slots):
+                at = cover_ref[block, slot]
+                live = slot < count_ref[block]
+                for kind in range(kinds):
+                    value = source_ref[at // cap, at % cap * kinds + kind]
+                    tiles.append(jnp.where(live, value, jnp.zeros_like(value)))
+            values.append(jnp.concatenate(tiles, axis=1))
+            tiles = [weight_ref[block, slot, kind] for slot in range(slots) for kind in range(kinds)]
+            weights.append(jnp.concatenate(tiles, axis=1))
         product = lax.dot_general(
-            jnp.concatenate(values, axis=1),
-            jnp.concatenate(weights, axis=1),
+            jnp.concatenate(values, axis=0),
+            jnp.concatenate(weights, axis=0),
             (((1,), (1,)), ((), ())),
             preferred_element_type=jnp.float32,
         )
-        results.append(product)
+        half = product.shape[1] // 2
+        results += [product[:ROWS, :half], product[ROWS:, half:]]
     remapped = jnp.concatenate(results, axis=1)
     cells = remapped.shape[1]
     coarse = remapped.astype(jnp.bfloat16)

time: 31 us -> 31.1 us (level)
  no operation moved by 1% of the time
where the time goes in v3:
time: 31.1 us; the launch traced here: 30.7 us
  starting transfers between devices  9.79 us (31%)
  blocking collectives  8.45 us (27%)
  Pallas kernels  7.66 us (25%)
  waiting for transfers between devices  4.78 us (15%)
    all_to_all x1, blocking collectives, swap(): lax.all_to_all(pieces, axis, split_axis=1, concat_axis=1, axis_index_grou...  8.45 us
    all_to_all x1, starting transfers between devices, shards(): lax.all_to_all(ordered, everyone, split_axis=0, concat_axis=0, tiled=True)  7.3 us
    ppermute x2, starting transfers between devices, send(): lax.ppermute(array, axis, [(at, at ^ apart) for at in range(lax.axis_size...  2.49 us
    all_to_all x1, waiting for transfers between devices, shards(): lax.all_to_all(ordered, everyone, split_axis=0, concat_axis=0, tiled=True)  2.47 us
    ppermute x2, waiting for transfers between devices, send(): lax.ppermute(array, axis, [(at, at ^ apart) for at in range(lax.axis_size...  2.31 us
    pallas_call x1, Pallas kernels, shards(): call(functools.partial(order_kernel, twins), shaped(messages, jnp.bfloat1...  2.14 us
    pallas_call x1, Pallas kernels, shards(): call(fetch_kernel, [shaped((DEPTH, ocean_cells), jnp.bfloat16), shaped(oc...  1.46 us
    pallas_call x1, Pallas kernels, shards(): call(select_kernel, [stencil] * twins, 'ahhhh', [pltpu.SMEM(send_list.sha...  0.98 us
  transfers between devices with their start and end apart: 3, of which 3 were waited for; matrix products, arithmetic and copies ran while one was open for 0% of the time, Pallas kernels for 10%

profile of v3, /device:TPU:0, one launch (start us, length us, event | category | flops | bytes accessed | tf_op | source)
XLA Modules:
  0.0 30.7 jit_solution(14487182003218070000)
XLA Ops:
  0.0 2.1 %shard_map.100.after_ref = bf16[768,128]{1,0:T(8,128)(2,1)} custom-call(s32[1,4096]{1,0:T(1,128)} %map_hbm.2, bf16[12,4096]{1,0:T(8,128)(2,1)} %flux_hbm.1), custom_call_target="tpu_custom_call" | custom-call | tf_op jit(solution)/shard_map/pallas_call | solution.py:341
  2.1 7.3 %all-to-all-start = ((bf16[32,24,128]{2,1,0:T(8,128)(2,1)}), bf16[32,24,128]{2,1,0:T(8,128)(2,1)S(1)}, u32[]{:S(2)}, u32[]{:S(2)}) async-start(bf16[32,24,128]{2,1,0:T(8,128)(2,1)} %bitcast), calls=%async_computation | async-start | bytes 393216 | tf_op jit(solution)/shard_map/all_to_all | solution.py:388
  9.5 1.0 %shard_map.102 = (f32[8,16,128]{2,1,0:T(8,128)S(1)}, f32[8,16,128]{2,1,0:T(8,128)S(1)}) custom-call(bf16[768,128]{1,0:T(8,128)(2,1)} %shard_map.100.after_ref, s32[1,4,4]{2,1,0:T(4,128)} %list_hbm.1, s32[4,4096]{1,0:T(4,128)} %near_hbm.1, f32[4,4096]{1,0:T(4,128)} %x_hbm.1, f32[4,4096]{1,0:T(4,128)} %y_hbm.1), custom_call_target="tpu_custom_call" | custom-call | bytes 3000000 | tf_op jit(solution)/shard_map/pallas_call | solution.py:356
  10.4 1.8 %collective-permute-start = (f32[8,16,128]{2,1,0:T(8,128)S(1)}, f32[8,16,128]{2,1,0:T(8,128)S(1)}, u32[]{:S(2)}, u32[]{:S(2)}) collective-permute-start(f32[8,16,128]{2,1,0:T(8,128)S(1)} %get-tuple-element.21), channel_id=1, source_target_pairs={{0,2},{1,3},{2,0},{3,1},{4,6},{5,7},{6,4},{7,5},{8,10},{9,11},{10,... | collective-permute-start | bytes 196616 | tf_op jit(solution)/shard_map/ppermute | solution.py:272
  12.3 1.5 %shard_map.101 = (bf16[256,512]{1,0:T(8,128)(2,1)S(1)}, s32[1,512]{1,0:T(1,128)S(1)}, s32[4,4]{1,0:T(4,128)S(4)}, s32[4]{0:T(128)S(4)}, bf16[4,4,3,128,128]{4,3,2,1,0:T(8,128)(2,1)S(1)}) custom-call(bf16[768,128]{1,0:T(8,128)(2,1)} %shard_map.100.after_ref, s32[1,512]{1,0:T(1,128)} %map_hbm.3, s32[4,4]{1,0:T(4,128)} %refs_0_.1, s32[4]{0:T(128)} %refs_1_.1, ...), custom_call_target="tpu_custom_call" | custom-call | bytes 3000000 | tf_op jit(solution)/shard_map/pallas_call | solution.py:372
  13.7 2.1 %collective-permute-done.refs_1_ = f32[8,16,128]{2,1,0:T(8,128)S(1)} collective-permute-done((f32[8,16,128]{2,1,0:T(8,128)S(1)}, f32[8,16,128]{2,1,0:T(8,128)S(1)}, u32[]{:S(2)}, u32[]{:S(2)}) %collective-permute-start) | collective-permute-done | bytes 65568 | tf_op jit(solution)/shard_map/ppermute | solution.py:272
  15.9 2.5 %all-to-all-done = bf16[32,24,128]{2,1,0:T(8,128)(2,1)S(1)} async-done(((bf16[32,24,128]{2,1,0:T(8,128)(2,1)}), bf16[32,24,128]{2,1,0:T(8,128)(2,1)S(1)}, u32[]{:S(2)}, u32[]{:S(2)}) %all-to-all-start) | async-done | bytes 196640 | tf_op jit(solution)/shard_map/all_to_all | solution.py:388
  18.3 0.9 %shard_map.103 = (bf16[2,12,16,128]{3,2,1,0:T(8,128)(2,1)S(1)}, bf16[2,256,256]{2,1,0:T(8,128)(2,1)S(1)}, f32[2,4,16,128]{3,2,1,0:T(8,128)S(1)}) custom-call(bf16[256,512]{1,0:T(8,128)(2,1)S(1)} %get-tuple-element.18.after_ref.moves_ref, bf16[768,128]{1,0:T(8,128)(2,1)S(1)} %bitcast.4, f32[8,16,128]{2,1,0:T(8,128)S(1)} %get-tuple-element.20.refs_0_, ...), custom_call_target="tpu_custom_call" | custom-call | flops 536870912 | tf_op jit(solution)/shard_map/pallas_call | solution.py:399
  19.2 0.7 %collective-permute-start.1 = (bf16[2,12,16,128]{3,2,1,0:T(8,128)(2,1)S(1)}, bf16[2,12,16,128]{3,2,1,0:T(8,128)(2,1)S(1)}, u32[]{:S(2)}, u32[]{:S(2)}) collective-permute-start(bf16[2,12,16,128]{3,2,1,0:T(8,128)(2,1)S(1)} %get-tuple-element.24), channel_id=1, source_target_pairs={{0,1},{1,0},{2,3},{3,2},{4,5},{5,4},{6,7},{7,6},{8,9},{9,8},{10,11... | collective-permute-start | bytes 294920 | tf_op jit(solution)/shard_map/ppermute | solution.py:272
  19.9 0.8 %shard_map.104.refs_0_ = bf16[2,12,16,128]{3,2,1,0:T(8,128)(2,1)S(1)} custom-call(bf16[2,256,256]{2,1,0:T(8,128)(2,1)S(1)} %get-tuple-element.22.tables, f32[2,4,16,128]{3,2,1,0:T(8,128)S(1)} %get-tuple-element.23.owns, f32[8,16,128]{2,1,0:T(8,128)S(1)} %get-tuple-element.20.refs_0_, f32[8,16,128]{2,1,0:T(8,128)S(1)} %collective-permute-done.refs_1_), custom_call_target="tpu_custom_call" | custom-call | flops 536870912 | bytes 4000000 | tf_op jit(solution)/shard_map/pallas_call | solution.py:406
  20.6 0.2 collective-permute-done.1.refs_1_
  20.8 0.8 %shard_map.105 = f32[8,8,128]{2,1,0:T(8,128)S(1)} custom-call(s32[4,4]{1,0:T(4,128)S(4)} %get-tuple-element.15.cover_ref, s32[4]{0:T(128)S(4)} %get-tuple-element.16.count_ref, bf16[4,4,3,128,128]{4,3,2,1,0:T(8,128)(2,1)S(1)} %get-tuple-element.17.weight_ref, bf16[256,512]{1,0:T(8,128)(2,1)S(1)} %get-tuple-element.18.after_ref.moves_ref, ...), custom_call_target="tpu_custom_call" | custom-call | tf_op jit(solution)/shard_map/pallas_call | solution.py:418
  21.6 8.5 %all_to_all.16 = f32[8,8,128]{2,0,1:T(8,128)S(1)} all-to-all(f32[8,8,128]{2,0,1:T(8,128)S(1)} %bitcast.5), channel_id=1, replica_groups={{16,12,20,8,24,4,28,0},{17,13,21,9,25,5,29,1},{18,14,22,10,26,6,30,2},{..., dimensions={1} | all-to-all | bytes 65536 | tf_op jit(solution)/shard_map/all_to_all | solution.py:282
  30.0 0.7 %shard_map.106 = f32[12,512]{1,0:T(8,128)} custom-call(f32[8,8,128]{2,1,0:T(8,128)S(1)} %bitcast.6), custom_call_target="tpu_custom_call" | custom-call | tf_op jit(solution)/shard_map/pallas_call | solution.py:426
Async XLA Ops:
  2.1 16.2 %all-to-all-start = ((bf16[32,24,128]{2,1,0:T(8,128)(2,1)}), bf16[32,24,128]{2,1,0:T(8,128)(2,1)S(1)}, u32[]{:S(2)}, u32[]{:S(2)}) async-start(bf16[32,24,128]{2,1,0:T(8,128)(2,1)} %bitcast), calls=%async_computation | async-start | bytes 393216 | tf_op jit(solution)/shard_map/all_to_all | solution.py:388
  10.4 5.4 %collective-permute-start = (f32[8,16,128]{2,1,0:T(8,128)S(1)}, f32[8,16,128]{2,1,0:T(8,128)S(1)}, u32[]{:S(2)}, u32[]{:S(2)}) collective-permute-start(f32[8,16,128]{2,1,0:T(8,128)S(1)} %get-tuple-element.21), channel_id=1, source_target_pairs={{0,2},{1,3},{2,0},{3,1},{4,6},{5,7},{6,4},{7,5},{8,10},{9,11},{10,... | collective-permute-start | bytes 196616 | tf_op jit(solution)/shard_map/ppermute | solution.py:272
  19.2 1.6 %collective-permute-start.1 = (bf16[2,12,16,128]{3,2,1,0:T(8,128)(2,1)S(1)}, bf16[2,12,16,128]{3,2,1,0:T(8,128)(2,1)S(1)}, u32[]{:S(2)}, u32[]{:S(2)}) collective-permute-start(bf16[2,12,16,128]{3,2,1,0:T(8,128)(2,1)S(1)} %get-tuple-element.24), channel_id=1, source_target_pairs={{0,1},{1,0},{2,3},{3,2},{4,5},{5,4},{6,7},{7,6},{8,9},{9,8},{10,11... | collective-permute-start | bytes 294920 | tf_op jit(solution)/shard_map/ppermute | solution.py:272

commit v4 on v2

--- a/solution.py
+++ b/solution.py
@@ -17,8 +17,11 @@
 VMEM_LIMIT = 40 * 1024 * 1024
 
 
-def one_hot(index):
-    row = lax.broadcasted_iota(jnp.int32, (DEPTH, index.shape[1]), 0).astype(jnp.bfloat16)
+def row_numbers(width):
+    return lax.broadcasted_iota(jnp.int32, (DEPTH, width), 0).astype(jnp.bfloat16)
+
+
+def one_hot(row, index):
     low = (index & (DEPTH - 1)).astype(jnp.bfloat16)
     return jnp.where(row == low, jnp.bfloat16(1), jnp.bfloat16(0))
 
@@ -31,20 +34,20 @@
     return result
 
 
-def lookup(table, index):
+def lookup(table, row_ref, index):
     results = []
     for at in range(0, index.shape[1], WIDTH):
         here = index[:, at : at + WIDTH]
-        found = jnp.dot(table, one_hot(here), preferred_element_type=jnp.float32)
+        found = jnp.dot(table, one_hot(row_ref[...], here), preferred_element_type=jnp.float32)
         results.append(choose(found, here // DEPTH, ROWS))
     return jnp.concatenate(results, axis=1)
 
 
-def lookup_dense(table, index, parts):
+def lookup_dense(table, row_ref, index, parts):
     results = []
     for at in range(0, index.shape[1], WIDTH):
         here = index[:, at : at + WIDTH]
-        found = jnp.dot(table, one_hot(here), preferred_element_type=jnp.float32)
+        found = jnp.dot(table, one_hot(row_ref[...], here), preferred_element_type=jnp.float32)
         high = here // DEPTH
         upper = choose(found[: HALF * parts], high, HALF)
         lower = choose(found[HALF * parts :], high // 2, HALF)
@@ -64,7 +67,7 @@
     return 2 * fields if twins == 2 else ROWS
 
 
-def order_kernel(twins, map_hbm, flux_hbm, out_hbm, map_ref, flux_ref, out_ref, table, sems):
+def order_kernel(twins, map_hbm, flux_hbm, out_hbm, map_ref, flux_ref, out_ref, table, row_ref, sems):
     fields, cells = flux_ref.shape
     steps = cells // STEP
     spans = [pl.ds(at, cells // 4) for at in range(0, cells, cells // 4)]
@@ -72,6 +75,7 @@
     needed += copies_of((map_hbm,), (map_ref,), sems, 4)
     for copy in needed:
         copy.start()
+    row_ref[...] = row_numbers(WIDTH)
     for copy in needed:
         copy.wait()
     parts, rest = cells // DEPTH, fields - HALF
@@ -82,7 +86,7 @@
     rows = message_rows(fields, twins)
     written = []
     for step in range(steps):
-        found = lookup_dense(table[...], map_ref[:, step * STEP : (step + 1) * STEP], parts)
+        found = lookup_dense(table[...], row_ref, map_ref[:, step * STEP : (step + 1) * STEP], parts)
         pieces = [found[:, at : at + LANES] for at in range(0, STEP, LANES)]
         if twins == 2:
             pieces = [
@@ -121,23 +125,25 @@
 
 
 def fetch_kernel(after_ref, map_hbm, *refs):
-    count = (len(refs) - 4) // 2
-    sources, (moves_ref, high_ref), targets, (map_ref, sems) = refs[:count], refs[count : count + 2], refs[count + 2 : -2], refs[-2:]
+    count = (len(refs) - 5) // 2
+    sources, (row_ref, moves_ref, high_ref) = refs[:count], refs[count : count + 3]
+    targets, (map_ref, sems) = refs[count + 3 : -2], refs[-2:]
     (needed,) = copies_of((map_hbm,), (map_ref,), sems, count)
     others = copies_of(sources, targets, sems)
     for copy in [needed] + others:
         copy.start()
     needed.wait()
-    moves_ref[...] = one_hot(map_ref[...])
+    row_ref[...] = row_numbers(WIDTH)
+    moves_ref[...] = one_hot(row_numbers(map_ref.shape[1]), map_ref[...])
     high_ref[...] = map_ref[...] // DEPTH
     for copy in others:
         copy.wait()
 
 
-def rebuild(near_count, table, stencil, own, shift):
+def rebuild(near_count, table, row_ref, stencil, own, shift):
     near = stencil[:near_count].astype(jnp.int32)
     index = jnp.concatenate([near[j : j + 1] for j in range(near_count)], axis=1)
-    found = lookup(table, index)
+    found = lookup(table, row_ref, index)
     upper = lower = own
     slope_x = slope_y = jnp.zeros_like(own)
     for j in range(near_count):
@@ -174,7 +180,7 @@
     return owns
 
 
-def outer_kernel(twins, near_count, fields, after_ref, cells_ref, *refs):
+def outer_kernel(twins, near_count, fields, row_ref, cells_ref, *refs):
     selected, refs = refs[:twins], refs[twins:]
     out_refs, (tables, owns) = refs[:-2], refs[-2:]
     cap = owns.shape[1]
@@ -190,18 +196,18 @@
                 owns[twin, at] = own
                 continue
             shift = twin * (fields - HALF)
-            results = rebuild(near_count, tables[twin], stencil_ref[at], own, shift)
+            results = rebuild(near_count, tables[twin], row_ref, stencil_ref[at], own, shift)
             for kind, result in enumerate(results):
                 out_refs[at // cap - 1][twin, at % cap * len(results) + kind] = result.astype(jnp.bfloat16)
 
 
-def inner_kernel(near_count, fields, tables, owns, *refs):
+def inner_kernel(near_count, fields, row_ref, tables, owns, *refs):
     selected, out_ref = refs[:-1], refs[-1]
     for twin, stencil_ref in enumerate(selected):
         for at in range(owns.shape[1]):
             own = owns[twin, at]
             shift = twin * (fields - HALF)
-            results = rebuild(near_count, tables[twin], stencil_ref[at], own, shift)
+            results = rebuild(near_count, tables[twin], row_ref, stencil_ref[at], own, shift)
             for kind, result in enumerate(results):
                 out_ref[twin, at * len(results) + kind] = result.astype(jnp.bfloat16)
 
@@ -344,6 +350,7 @@
             scratch(atm_flux),
             pltpu.VMEM(messages, jnp.bfloat16),
             pltpu.VMEM((cells // DEPTH * fields, DEPTH), jnp.bfloat16),
+            pltpu.VMEM((DEPTH, WIDTH), jnp.bfloat16),
             pltpu.SemaphoreType.DMA((cells // STEP + 5,)),
         ],
         out_memory="h",
@@ -366,9 +373,10 @@
     selected = [selected[0]] + [send(array, "local", 2) for array in selected[1:]]
 
     later = [cover, cover_count, weights]
-    moves, high, cover, cover_count, weights = call(
+    row, moves, high, cover, cover_count, weights = call(
         fetch_kernel,
         [
+            shaped((DEPTH, WIDTH), jnp.bfloat16),
             shaped((DEPTH, ocean_cells), jnp.bfloat16),
             shaped(ocean_map.shape, ocean_map.dtype),
             pltpu.SMEM(cover.shape, cover.dtype),
@@ -377,7 +385,7 @@
         ],
         "ah" + "h" * len(later),
         [scratch(ocean_map), pltpu.SemaphoreType.DMA((len(later) + 1,))],
-        out_memory="vvssv",
+        out_memory="vvvssv",
         moved=3_000_000,
     )(ordered, *stay(ocean_map, *later))
 
@@ -396,17 +404,17 @@
     *outer, tables, owns = call(
         functools.partial(outer_kernel, twins, near_count, fields),
         [sent] * (aparts - 1) + [tables, owns],
-        "av" + "v" * twins,
+        "vv" + "v" * twins,
         flops=work * (aparts - 1),
-    )(moves, coupled, *selected)
+    )(row, coupled, *selected)
     source = [send(array, "local", 1 + at) for at, array in enumerate(outer)]
     inner = call(
         functools.partial(inner_kernel, near_count, fields),
         sent,
-        "vv" + "v" * twins,
+        "vvv" + "v" * twins,
         flops=work,
         moved=4_000_000,
-    )(tables, owns, *selected)
+    )(row, tables, owns, *selected)
     source = [inner] + source
 
     share = ocean_cells // region_count

time: 31 us -> 31.1 us (level)
  no operation moved by 1% of the time
where the time goes in v4:
time: 31.1 us; the launch traced here: 30.7 us
  starting transfers between devices  9.79 us (31%)
  blocking collectives  8.45 us (27%)
  Pallas kernels  7.68 us (25%)
  waiting for transfers between devices  4.77 us (15%)
    all_to_all x1, blocking collectives, swap(): lax.all_to_all(pieces, axis, split_axis=1, concat_axis=1, axis_index_grou...  8.45 us
    all_to_all x1, starting transfers between devices, shards(): lax.all_to_all(ordered, everyone, split_axis=0, concat_axis=0, tiled=True)  7.3 us
    ppermute x2, starting transfers between devices, send(): lax.ppermute(array, axis, [(at, at ^ apart) for at in range(lax.axis_size...  2.49 us
    all_to_all x1, waiting for transfers between devices, shards(): lax.all_to_all(ordered, everyone, split_axis=0, concat_axis=0, tiled=True)  2.47 us
    ppermute x2, waiting for transfers between devices, send(): lax.ppermute(array, axis, [(at, at ^ apart) for at in range(lax.axis_size...  2.3 us
    pallas_call x1, Pallas kernels, shards(): call(functools.partial(order_kernel, twins), shaped(messages, jnp.bfloat1...  2.21 us
    pallas_call x1, Pallas kernels, shards(): call(fetch_kernel, [shaped((DEPTH, WIDTH), jnp.bfloat16), shaped((DEPTH,...  1.46 us
    pallas_call x1, Pallas kernels, shards(): call(select_kernel, [stencil] * twins, 'ahhhh', [pltpu.SMEM(send_list.sha...  0.98 us
  transfers between devices with their start and end apart: 3, of which 3 were waited for; matrix products, arithmetic and copies ran while one was open for 0% of the time, Pallas kernels for 10%

profile of v4, /device:TPU:0, one launch (start us, length us, event | category | flops | bytes accessed | tf_op | source)
XLA Modules:
  0.0 30.7 jit_solution(1370662539853997331)
XLA Ops:
  0.0 2.2 %shard_map.100.after_ref = bf16[768,128]{1,0:T(8,128)(2,1)} custom-call(s32[1,4096]{1,0:T(1,128)} %map_hbm.2, bf16[12,4096]{1,0:T(8,128)(2,1)} %flux_hbm.1), custom_call_target="tpu_custom_call" | custom-call | tf_op jit(solution)/shard_map/pallas_call | solution.py:344
  2.2 7.3 %all-to-all-start = ((bf16[32,24,128]{2,1,0:T(8,128)(2,1)}), bf16[32,24,128]{2,1,0:T(8,128)(2,1)S(1)}, u32[]{:S(2)}, u32[]{:S(2)}) async-start(bf16[32,24,128]{2,1,0:T(8,128)(2,1)} %bitcast), calls=%async_computation | async-start | bytes 393216 | tf_op jit(solution)/shard_map/all_to_all | solution.py:393
  9.5 1.0 %shard_map.102 = (f32[8,16,128]{2,1,0:T(8,128)S(1)}, f32[8,16,128]{2,1,0:T(8,128)S(1)}) custom-call(bf16[768,128]{1,0:T(8,128)(2,1)} %shard_map.100.after_ref, s32[1,4,4]{2,1,0:T(4,128)} %list_hbm.1, s32[4,4096]{1,0:T(4,128)} %near_hbm.1, f32[4,4096]{1,0:T(4,128)} %x_hbm.1, f32[4,4096]{1,0:T(4,128)} %y_hbm.1), custom_call_target="tpu_custom_call" | custom-call | bytes 3000000 | tf_op jit(solution)/shard_map/pallas_call | solution.py:360
  10.5 1.8 %collective-permute-start = (f32[8,16,128]{2,1,0:T(8,128)S(1)}, f32[8,16,128]{2,1,0:T(8,128)S(1)}, u32[]{:S(2)}, u32[]{:S(2)}) collective-permute-start(f32[8,16,128]{2,1,0:T(8,128)S(1)} %get-tuple-element.23), channel_id=1, source_target_pairs={{0,2},{1,3},{2,0},{3,1},{4,6},{5,7},{6,4},{7,5},{8,10},{9,11},{10,... | collective-permute-start | bytes 196616 | tf_op jit(solution)/shard_map/ppermute | solution.py:275
  12.3 1.5 %shard_map.101 = (bf16[256,256]{1,0:T(8,128)(2,1)S(1)}, bf16[256,512]{1,0:T(8,128)(2,1)S(1)}, s32[1,512]{1,0:T(1,128)S(1)}, s32[4,4]{1,0:T(4,128)S(4)}, s32[4]{0...) custom-call(bf16[768,128]{1,0:T(8,128)(2,1)} %shard_map.100.after_ref, s32[1,512]{1,0:T(1,128)} %map_hbm.3, ...), custom_call_target="tpu_custom_call" | custom-call | bytes 3000000 | tf_op jit(solution)/shard_map/pallas_call | solution.py:376
  13.8 2.1 %collective-permute-done.refs_1_ = f32[8,16,128]{2,1,0:T(8,128)S(1)} collective-permute-done((f32[8,16,128]{2,1,0:T(8,128)S(1)}, f32[8,16,128]{2,1,0:T(8,128)S(1)}, u32[]{:S(2)}, u32[]{:S(2)}) %collective-permute-start) | collective-permute-done | bytes 65568 | tf_op jit(solution)/shard_map/ppermute | solution.py:275
  15.9 2.5 %all-to-all-done = bf16[32,24,128]{2,1,0:T(8,128)(2,1)S(1)} async-done(((bf16[32,24,128]{2,1,0:T(8,128)(2,1)}), bf16[32,24,128]{2,1,0:T(8,128)(2,1)S(1)}, u32[]{:S(2)}, u32[]{:S(2)}) %all-to-all-start) | async-done | bytes 196640 | tf_op jit(solution)/shard_map/all_to_all | solution.py:393
  18.4 0.9 %shard_map.103 = (bf16[2,12,16,128]{3,2,1,0:T(8,128)(2,1)S(1)}, bf16[2,256,256]{2,1,0:T(8,128)(2,1)S(1)}, f32[2,4,16,128]{3,2,1,0:T(8,128)S(1)}) custom-call(bf16[256,256]{1,0:T(8,128)(2,1)S(1)} %get-tuple-element.21.row_ref, bf16[768,128]{1,0:T(8,128)(2,1)S(1)} %bitcast.4, f32[8,16,128]{2,1,0:T(8,128)S(1)} %get-tuple-element.22.refs_0_, ...), custom_call_target="tpu_custom_call" | custom-call | flops 536870912 | tf_op jit(solution)/shard_map/pallas_call | solution.py:404
  19.3 0.7 %collective-permute-start.1 = (bf16[2,12,16,128]{3,2,1,0:T(8,128)(2,1)S(1)}, bf16[2,12,16,128]{3,2,1,0:T(8,128)(2,1)S(1)}, u32[]{:S(2)}, u32[]{:S(2)}) collective-permute-start(bf16[2,12,16,128]{3,2,1,0:T(8,128)(2,1)S(1)} %get-tuple-element.26), channel_id=1, source_target_pairs={{0,1},{1,0},{2,3},{3,2},{4,5},{5,4},{6,7},{7,6},{8,9},{9,8},{10,11... | collective-permute-start | bytes 294920 | tf_op jit(solution)/shard_map/ppermute | solution.py:275
  19.9 0.8 %shard_map.104.refs_0_ = bf16[2,12,16,128]{3,2,1,0:T(8,128)(2,1)S(1)} custom-call(bf16[256,256]{1,0:T(8,128)(2,1)S(1)} %get-tuple-element.21.row_ref, bf16[2,256,256]{2,1,0:T(8,128)(2,1)S(1)} %get-tuple-element.24.tables, f32[2,4,16,128]{3,2,1,0:T(8,128)S(1)} %get-tuple-element.25.owns, f32[8,16,128]{2,1,0:T(8,128)S(1)} %get-tuple-element.22.refs_0_, ...), custom_call_target="tpu_custom_call" | custom-call | flops 536870912 | bytes 4000000 | tf_op jit(solution)/shard_map/pallas_call | solution.py:411
  20.7 0.2 collective-permute-done.1.refs_1_
  20.9 0.7 %shard_map.105 = f32[8,8,128]{2,1,0:T(8,128)S(1)} custom-call(s32[4,4]{1,0:T(4,128)S(4)} %get-tuple-element.16.cover_ref, s32[4]{0:T(128)S(4)} %get-tuple-element.17.count_ref, bf16[4,4,3,128,128]{4,3,2,1,0:T(8,128)(2,1)S(1)} %get-tuple-element.18.weight_ref, bf16[256,512]{1,0:T(8,128)(2,1)S(1)} %get-tuple-element.19.moves_ref, ...), custom_call_target="tpu_custom_call" | custom-call | tf_op jit(solution)/shard_map/pallas_call | solution.py:423
  21.6 8.5 %all_to_all.16 = f32[8,8,128]{2,0,1:T(8,128)S(1)} all-to-all(f32[8,8,128]{2,0,1:T(8,128)S(1)} %bitcast.5), channel_id=1, replica_groups={{16,12,20,8,24,4,28,0},{17,13,21,9,25,5,29,1},{18,14,22,10,26,6,30,2},{..., dimensions={1} | all-to-all | bytes 65536 | tf_op jit(solution)/shard_map/all_to_all | solution.py:285
  30.0 0.7 %shard_map.106 = f32[12,512]{1,0:T(8,128)} custom-call(f32[8,8,128]{2,1,0:T(8,128)S(1)} %bitcast.6), custom_call_target="tpu_custom_call" | custom-call | tf_op jit(solution)/shard_map/pallas_call | solution.py:431
Async XLA Ops:
  2.2 16.2 %all-to-all-start = ((bf16[32,24,128]{2,1,0:T(8,128)(2,1)}), bf16[32,24,128]{2,1,0:T(8,128)(2,1)S(1)}, u32[]{:S(2)}, u32[]{:S(2)}) async-start(bf16[32,24,128]{2,1,0:T(8,128)(2,1)} %bitcast), calls=%async_computation | async-start | bytes 393216 | tf_op jit(solution)/shard_map/all_to_all | solution.py:393
  10.5 5.4 %collective-permute-start = (f32[8,16,128]{2,1,0:T(8,128)S(1)}, f32[8,16,128]{2,1,0:T(8,128)S(1)}, u32[]{:S(2)}, u32[]{:S(2)}) collective-permute-start(f32[8,16,128]{2,1,0:T(8,128)S(1)} %get-tuple-element.23), channel_id=1, source_target_pairs={{0,2},{1,3},{2,0},{3,1},{4,6},{5,7},{6,4},{7,5},{8,10},{9,11},{10,... | collective-permute-start | bytes 196616 | tf_op jit(solution)/shard_map/ppermute | solution.py:275
  19.3 1.6 %collective-permute-start.1 = (bf16[2,12,16,128]{3,2,1,0:T(8,128)(2,1)S(1)}, bf16[2,12,16,128]{3,2,1,0:T(8,128)(2,1)S(1)}, u32[]{:S(2)}, u32[]{:S(2)}) collective-permute-start(bf16[2,12,16,128]{3,2,1,0:T(8,128)(2,1)S(1)} %get-tuple-element.26), channel_id=1, source_target_pairs={{0,1},{1,0},{2,3},{3,2},{4,5},{5,4},{6,7},{7,6},{8,9},{9,8},{10,11... | collective-permute-start | bytes 294920 | tf_op jit(solution)/shard_map/ppermute | solution.py:275

commit v5 on v2

--- a/solution.py
+++ b/solution.py
@@ -18,8 +18,8 @@
 
 
 def one_hot(index):
-    row = lax.broadcasted_iota(jnp.int32, (DEPTH, index.shape[1]), 0).astype(jnp.bfloat16)
-    low = (index & (DEPTH - 1)).astype(jnp.bfloat16)
+    row = lax.broadcasted_iota(jnp.int32, (DEPTH, index.shape[1]), 0).astype(jnp.int16)
+    low = (index & (DEPTH - 1)).astype(jnp.int16)
     return jnp.where(row == low, jnp.bfloat16(1), jnp.bfloat16(0))
 
 

time: 31 us -> 31 us (level)
  no operation moved by 1% of the time
where the time goes in v5:
time: 31 us; the launch traced here: 30.6 us
  starting transfers between devices  9.8 us (32%)
  blocking collectives  8.45 us (27%)
  Pallas kernels  7.51 us (24%)
  waiting for transfers between devices  4.8 us (15%)
    all_to_all x1, blocking collectives, swap(): lax.all_to_all(pieces, axis, split_axis=1, concat_axis=1, axis_index_grou...  8.45 us
    all_to_all x1, starting transfers between devices, shards(): lax.all_to_all(ordered, everyone, split_axis=0, concat_axis=0, tiled=True)  7.3 us
    ppermute x2, starting transfers between devices, send(): lax.ppermute(array, axis, [(at, at ^ apart) for at in range(lax.axis_size...  2.49 us
    all_to_all x1, waiting for transfers between devices, shards(): lax.all_to_all(ordered, everyone, split_axis=0, concat_axis=0, tiled=True)  2.47 us
    ppermute x2, waiting for transfers between devices, send(): lax.ppermute(array, axis, [(at, at ^ apart) for at in range(lax.axis_size...  2.34 us
    pallas_call x1, Pallas kernels, shards(): call(functools.partial(order_kernel, twins), shaped(messages, jnp.bfloat1...  2.13 us
    pallas_call x1, Pallas kernels, shards(): call(fetch_kernel, [shaped((DEPTH, ocean_cells), jnp.bfloat16), shaped(oc...  1.46 us
    pallas_call x1, Pallas kernels, shards(): call(select_kernel, [stencil] * twins, 'ahhhh', [pltpu.SMEM(send_list.sha...  0.98 us
  transfers between devices with their start and end apart: 3, of which 3 were waited for; matrix products, arithmetic and copies ran while one was open for 0% of the time, Pallas kernels for 10%

profile of v5, /device:TPU:0, one launch (start us, length us, event | category | flops | bytes accessed | tf_op | source)
XLA Modules:
  0.0 30.6 jit_solution(17971637077918131224)
XLA Ops:
  0.0 2.1 %shard_map.100.after_ref = bf16[768,128]{1,0:T(8,128)(2,1)} custom-call(s32[1,4096]{1,0:T(1,128)} %map_hbm.2, bf16[12,4096]{1,0:T(8,128)(2,1)} %flux_hbm.1), custom_call_target="tpu_custom_call" | custom-call | tf_op jit(solution)/shard_map/pallas_call | solution.py:338
  2.1 7.3 %all-to-all-start = ((bf16[32,24,128]{2,1,0:T(8,128)(2,1)}), bf16[32,24,128]{2,1,0:T(8,128)(2,1)S(1)}, u32[]{:S(2)}, u32[]{:S(2)}) async-start(bf16[32,24,128]{2,1,0:T(8,128)(2,1)} %bitcast), calls=%async_computation | async-start | bytes 393216 | tf_op jit(solution)/shard_map/all_to_all | solution.py:385
  9.5 1.0 %shard_map.102 = (f32[8,16,128]{2,1,0:T(8,128)S(1)}, f32[8,16,128]{2,1,0:T(8,128)S(1)}) custom-call(bf16[768,128]{1,0:T(8,128)(2,1)} %shard_map.100.after_ref, s32[1,4,4]{2,1,0:T(4,128)} %list_hbm.1, s32[4,4096]{1,0:T(4,128)} %near_hbm.1, f32[4,4096]{1,0:T(4,128)} %x_hbm.1, f32[4,4096]{1,0:T(4,128)} %y_hbm.1), custom_call_target="tpu_custom_call" | custom-call | bytes 3000000 | tf_op jit(solution)/shard_map/pallas_call | solution.py:353
  10.4 1.8 %collective-permute-start = (f32[8,16,128]{2,1,0:T(8,128)S(1)}, f32[8,16,128]{2,1,0:T(8,128)S(1)}, u32[]{:S(2)}, u32[]{:S(2)}) collective-permute-start(f32[8,16,128]{2,1,0:T(8,128)S(1)} %get-tuple-element.21), channel_id=1, source_target_pairs={{0,2},{1,3},{2,0},{3,1},{4,6},{5,7},{6,4},{7,5},{8,10},{9,11},{10,... | collective-permute-start | bytes 196616 | tf_op jit(solution)/shard_map/ppermute | solution.py:269
  12.3 1.5 %shard_map.101 = (bf16[256,512]{1,0:T(8,128)(2,1)S(1)}, s32[1,512]{1,0:T(1,128)S(1)}, s32[4,4]{1,0:T(4,128)S(4)}, s32[4]{0:T(128)S(4)}, bf16[4,4,3,128,128]{4,3,2,1,0:T(8,128)(2,1)S(1)}) custom-call(bf16[768,128]{1,0:T(8,128)(2,1)} %shard_map.100.after_ref, s32[1,512]{1,0:T(1,128)} %map_hbm.3, s32[4,4]{1,0:T(4,128)} %refs_0_.1, s32[4]{0:T(128)} %refs_1_.1, ...), custom_call_target="tpu_custom_call" | custom-call | bytes 3000000 | tf_op jit(solution)/shard_map/pallas_call | solution.py:369
  13.7 2.1 %collective-permute-done.refs_1_ = f32[8,16,128]{2,1,0:T(8,128)S(1)} collective-permute-done((f32[8,16,128]{2,1,0:T(8,128)S(1)}, f32[8,16,128]{2,1,0:T(8,128)S(1)}, u32[]{:S(2)}, u32[]{:S(2)}) %collective-permute-start) | collective-permute-done | bytes 65568 | tf_op jit(solution)/shard_map/ppermute | solution.py:269
  15.9 2.5 %all-to-all-done = bf16[32,24,128]{2,1,0:T(8,128)(2,1)S(1)} async-done(((bf16[32,24,128]{2,1,0:T(8,128)(2,1)}), bf16[32,24,128]{2,1,0:T(8,128)(2,1)S(1)}, u32[]{:S(2)}, u32[]{:S(2)}) %all-to-all-start) | async-done | bytes 196640 | tf_op jit(solution)/shard_map/all_to_all | solution.py:385
  18.3 0.8 %shard_map.103 = (bf16[2,12,16,128]{3,2,1,0:T(8,128)(2,1)S(1)}, bf16[2,256,256]{2,1,0:T(8,128)(2,1)S(1)}, f32[2,4,16,128]{3,2,1,0:T(8,128)S(1)}) custom-call(bf16[256,512]{1,0:T(8,128)(2,1)S(1)} %get-tuple-element.18.after_ref.moves_ref, bf16[768,128]{1,0:T(8,128)(2,1)S(1)} %bitcast.4, f32[8,16,128]{2,1,0:T(8,128)S(1)} %get-tuple-element.20.refs_0_, ...), custom_call_target="tpu_custom_call" | custom-call | flops 536870912 | tf_op jit(solution)/shard_map/pallas_call | solution.py:396
  19.1 0.7 %collective-permute-start.1 = (bf16[2,12,16,128]{3,2,1,0:T(8,128)(2,1)S(1)}, bf16[2,12,16,128]{3,2,1,0:T(8,128)(2,1)S(1)}, u32[]{:S(2)}, u32[]{:S(2)}) collective-permute-start(bf16[2,12,16,128]{3,2,1,0:T(8,128)(2,1)S(1)} %get-tuple-element.24), channel_id=1, source_target_pairs={{0,1},{1,0},{2,3},{3,2},{4,5},{5,4},{6,7},{7,6},{8,9},{9,8},{10,11... | collective-permute-start | bytes 294920 | tf_op jit(solution)/shard_map/ppermute | solution.py:269
  19.8 0.7 %shard_map.104.refs_0_ = bf16[2,12,16,128]{3,2,1,0:T(8,128)(2,1)S(1)} custom-call(bf16[2,256,256]{2,1,0:T(8,128)(2,1)S(1)} %get-tuple-element.22.tables, f32[2,4,16,128]{3,2,1,0:T(8,128)S(1)} %get-tuple-element.23.owns, f32[8,16,128]{2,1,0:T(8,128)S(1)} %get-tuple-element.20.refs_0_, f32[8,16,128]{2,1,0:T(8,128)S(1)} %collective-permute-done.refs_1_), custom_call_target="tpu_custom_call" | custom-call | flops 536870912 | bytes 4000000 | tf_op jit(solution)/shard_map/pallas_call | solution.py:403
  20.5 0.2 collective-permute-done.1.refs_1_
  20.7 0.7 %shard_map.105 = f32[8,8,128]{2,1,0:T(8,128)S(1)} custom-call(s32[4,4]{1,0:T(4,128)S(4)} %get-tuple-element.15.cover_ref, s32[4]{0:T(128)S(4)} %get-tuple-element.16.count_ref, bf16[4,4,3,128,128]{4,3,2,1,0:T(8,128)(2,1)S(1)} %get-tuple-element.17.weight_ref, bf16[256,512]{1,0:T(8,128)(2,1)S(1)} %get-tuple-element.18.after_ref.moves_ref, ...), custom_call_target="tpu_custom_call" | custom-call | tf_op jit(solution)/shard_map/pallas_call | solution.py:415
  21.5 8.4 %all_to_all.16 = f32[8,8,128]{2,0,1:T(8,128)S(1)} all-to-all(f32[8,8,128]{2,0,1:T(8,128)S(1)} %bitcast.5), channel_id=1, replica_groups={{16,12,20,8,24,4,28,0},{17,13,21,9,25,5,29,1},{18,14,22,10,26,6,30,2},{..., dimensions={1} | all-to-all | bytes 65536 | tf_op jit(solution)/shard_map/all_to_all | solution.py:279
  29.9 0.7 %shard_map.106 = f32[12,512]{1,0:T(8,128)} custom-call(f32[8,8,128]{2,1,0:T(8,128)S(1)} %bitcast.6), custom_call_target="tpu_custom_call" | custom-call | tf_op jit(solution)/shard_map/pallas_call | solution.py:423
Async XLA Ops:
  2.1 16.2 %all-to-all-start = ((bf16[32,24,128]{2,1,0:T(8,128)(2,1)}), bf16[32,24,128]{2,1,0:T(8,128)(2,1)S(1)}, u32[]{:S(2)}, u32[]{:S(2)}) async-start(bf16[32,24,128]{2,1,0:T(8,128)(2,1)} %bitcast), calls=%async_computation | async-start | bytes 393216 | tf_op jit(solution)/shard_map/all_to_all | solution.py:385
  10.4 5.4 %collective-permute-start = (f32[8,16,128]{2,1,0:T(8,128)S(1)}, f32[8,16,128]{2,1,0:T(8,128)S(1)}, u32[]{:S(2)}, u32[]{:S(2)}) collective-permute-start(f32[8,16,128]{2,1,0:T(8,128)S(1)} %get-tuple-element.21), channel_id=1, source_target_pairs={{0,2},{1,3},{2,0},{3,1},{4,6},{5,7},{6,4},{7,5},{8,10},{9,11},{10,... | collective-permute-start | bytes 196616 | tf_op jit(solution)/shard_map/ppermute | solution.py:269
  19.1 1.6 %collective-permute-start.1 = (bf16[2,12,16,128]{3,2,1,0:T(8,128)(2,1)S(1)}, bf16[2,12,16,128]{3,2,1,0:T(8,128)(2,1)S(1)}, u32[]{:S(2)}, u32[]{:S(2)}) collective-permute-start(bf16[2,12,16,128]{3,2,1,0:T(8,128)(2,1)S(1)} %get-tuple-element.24), channel_id=1, source_target_pairs={{0,1},{1,0},{2,3},{3,2},{4,5},{5,4},{6,7},{7,6},{8,9},{9,8},{10,11... | collective-permute-start | bytes 294920 | tf_op jit(solution)/shard_map/ppermute | solution.py:269

commit v6 on v2

--- a/solution.py
+++ b/solution.py
@@ -12,7 +12,7 @@
 LANES = 128
 DEPTH = 256
 PER_ROW = DEPTH // LANES
-STEP = 512
+STEP = 1024
 WIDTH = 256
 VMEM_LIMIT = 40 * 1024 * 1024
 
@@ -67,9 +67,7 @@
 def order_kernel(twins, map_hbm, flux_hbm, out_hbm, map_ref, flux_ref, out_ref, table, sems):
     fields, cells = flux_ref.shape
     steps = cells // STEP
-    spans = [pl.ds(at, cells // 4) for at in range(0, cells, cells // 4)]
-    needed = copies_of([flux_hbm.at[:, span] for span in spans], [flux_ref.at[:, span] for span in spans], sems)
-    needed += copies_of((map_hbm,), (map_ref,), sems, 4)
+    needed = copies_of((map_hbm, flux_hbm), (map_ref, flux_ref), sems)
     for copy in needed:
         copy.start()
     for copy in needed:
@@ -92,7 +90,7 @@
             first = (step * len(pieces) + at) * rows
             out_ref[first : first + rows] = piece.astype(jnp.bfloat16)
         span = pl.ds(step * len(pieces) * rows, len(pieces) * rows)
-        written.append(pltpu.make_async_copy(out_ref.at[span], out_hbm.at[span], sems.at[5 + step]))
+        written.append(pltpu.make_async_copy(out_ref.at[span], out_hbm.at[span], sems.at[2 + step]))
         written[-1].start()
     for copy in written:
         copy.wait()
@@ -207,21 +205,22 @@
 
 
 def remap_kernel(packed, fields, cover_ref, count_ref, weight_ref, moves_ref, high_ref, *refs):
-    received, (out_ref, source_ref) = refs[:-2], refs[-2:]
+    received, out_ref = refs[:-1], refs[-1]
     me = lax.axis_index("local")
     ocean_blocks, slots, kinds = weight_ref.shape[:3]
-    cap = source_ref.shape[1] // kinds
-    for apart, piece_ref in enumerate(received):
-        for twin in range(piece_ref.shape[0]):
-            source_ref[me ^ apart ^ (2 * twin)] = piece_ref[twin]
+    cap = received[0].shape[1] // kinds
     results = []
     for block in range(ocean_blocks):
         values, weights = [], []
         for slot in range(slots):
             at = cover_ref[block, slot]
             live = slot < count_ref[block]
+            apart = me ^ (at // cap)
+            twin, apart = apart // len(received), apart % len(received)
             for kind in range(kinds):
-                value = source_ref[at // cap, at % cap * kinds + kind]
+                value = received[0][twin, at % cap * kinds + kind]
+                for other in range(1, len(received)):
+                    value = jnp.where(apart == other, received[other][twin, at % cap * kinds + kind], value)
                 values.append(jnp.where(live, value, jnp.zeros_like(value)))
                 weights.append(weight_ref[block, slot, kind])
         product = lax.dot_general(
@@ -344,7 +343,7 @@
             scratch(atm_flux),
             pltpu.VMEM(messages, jnp.bfloat16),
             pltpu.VMEM((cells // DEPTH * fields, DEPTH), jnp.bfloat16),
-            pltpu.SemaphoreType.DMA((cells // STEP + 5,)),
+            pltpu.SemaphoreType.DMA((cells // STEP + 2,)),
         ],
         out_memory="h",
     )(*stay(cell_map, atm_flux))
@@ -416,7 +415,6 @@
         functools.partial(remap_kernel, packed, fields),
         shaped(out_shape, jnp.float32),
         "ssvvv" + "v" * aparts,
-        [pltpu.VMEM((local_count, cap * kinds, ROWS, LANES), jnp.bfloat16)],
     )(cover, cover_count, weights, moves, high, *source)
     if packed:
         landed = swap(leaving, "region")

time: 31 us -> 31 us (level)
  no operation moved by 1% of the time
where the time goes in v6:
time: 31 us; the launch traced here: 30.7 us
  starting transfers between devices  9.8 us (32%)
  blocking collectives  8.45 us (27%)
  Pallas kernels  7.6 us (25%)
  waiting for transfers between devices  4.8 us (15%)
    all_to_all x1, blocking collectives, swap(): lax.all_to_all(pieces, axis, split_axis=1, concat_axis=1, axis_index_grou...  8.45 us
    all_to_all x1, starting transfers between devices, shards(): lax.all_to_all(ordered, everyone, split_axis=0, concat_axis=0, tiled=True)  7.31 us
    ppermute x2, starting transfers between devices, send(): lax.ppermute(array, axis, [(at, at ^ apart) for at in range(lax.axis_size...  2.49 us
    all_to_all x1, waiting for transfers between devices, shards(): lax.all_to_all(ordered, everyone, split_axis=0, concat_axis=0, tiled=True)  2.47 us
    ppermute x2, waiting for transfers between devices, send(): lax.ppermute(array, axis, [(at, at ^ apart) for at in range(lax.axis_size...  2.33 us
    pallas_call x1, Pallas kernels, shards(): call(functools.partial(order_kernel, twins), shaped(messages, jnp.bfloat1...  2.21 us
    pallas_call x1, Pallas kernels, shards(): call(fetch_kernel, [shaped((DEPTH, ocean_cells), jnp.bfloat16), shaped(oc...  1.46 us
    pallas_call x1, Pallas kernels, shards(): call(select_kernel, [stencil] * twins, 'ahhhh', [pltpu.SMEM(send_list.sha...  0.98 us
  transfers between devices with their start and end apart: 3, of which 3 were waited for; matrix products, arithmetic and copies ran while one was open for 0% of the time, Pallas kernels for 10%

profile of v6, /device:TPU:0, one launch (start us, length us, event | category | flops | bytes accessed | tf_op | source)
XLA Modules:
  0.0 30.7 jit_solution(4049193155827702778)
XLA Ops:
  0.0 2.2 %shard_map.100.after_ref = bf16[768,128]{1,0:T(8,128)(2,1)} custom-call(s32[1,4096]{1,0:T(1,128)} %map_hbm.2, bf16[12,4096]{1,0:T(8,128)(2,1)} %flux_hbm.1), custom_call_target="tpu_custom_call" | custom-call | tf_op jit(solution)/shard_map/pallas_call | solution.py:337
  2.2 7.3 %all-to-all-start = ((bf16[32,24,128]{2,1,0:T(8,128)(2,1)}), bf16[32,24,128]{2,1,0:T(8,128)(2,1)S(1)}, u32[]{:S(2)}, u32[]{:S(2)}) async-start(bf16[32,24,128]{2,1,0:T(8,128)(2,1)} %bitcast), calls=%async_computation | async-start | bytes 393216 | tf_op jit(solution)/shard_map/all_to_all | solution.py:384
  9.5 1.0 %shard_map.102 = (f32[8,16,128]{2,1,0:T(8,128)S(1)}, f32[8,16,128]{2,1,0:T(8,128)S(1)}) custom-call(bf16[768,128]{1,0:T(8,128)(2,1)} %shard_map.100.after_ref, s32[1,4,4]{2,1,0:T(4,128)} %list_hbm.1, s32[4,4096]{1,0:T(4,128)} %near_hbm.1, f32[4,4096]{1,0:T(4,128)} %x_hbm.1, f32[4,4096]{1,0:T(4,128)} %y_hbm.1), custom_call_target="tpu_custom_call" | custom-call | bytes 3000000 | tf_op jit(solution)/shard_map/pallas_call | solution.py:352
  10.5 1.8 %collective-permute-start = (f32[8,16,128]{2,1,0:T(8,128)S(1)}, f32[8,16,128]{2,1,0:T(8,128)S(1)}, u32[]{:S(2)}, u32[]{:S(2)}) collective-permute-start(f32[8,16,128]{2,1,0:T(8,128)S(1)} %get-tuple-element.21), channel_id=1, source_target_pairs={{0,2},{1,3},{2,0},{3,1},{4,6},{5,7},{6,4},{7,5},{8,10},{9,11},{10,... | collective-permute-start | bytes 196616 | tf_op jit(solution)/shard_map/ppermute | solution.py:268
  12.4 1.5 %shard_map.101 = (bf16[256,512]{1,0:T(8,128)(2,1)S(1)}, s32[1,512]{1,0:T(1,128)S(1)}, s32[4,4]{1,0:T(4,128)S(4)}, s32[4]{0:T(128)S(4)}, bf16[4,4,3,128,128]{4,3,2,1,0:T(8,128)(2,1)S(1)}) custom-call(bf16[768,128]{1,0:T(8,128)(2,1)} %shard_map.100.after_ref, s32[1,512]{1,0:T(1,128)} %map_hbm.3, s32[4,4]{1,0:T(4,128)} %refs_0_.1, s32[4]{0:T(128)} %refs_1_.1, ...), custom_call_target="tpu_custom_call" | custom-call | bytes 3000000 | tf_op jit(solution)/shard_map/pallas_call | solution.py:368
  13.8 2.1 %collective-permute-done.refs_1_ = f32[8,16,128]{2,1,0:T(8,128)S(1)} collective-permute-done((f32[8,16,128]{2,1,0:T(8,128)S(1)}, f32[8,16,128]{2,1,0:T(8,128)S(1)}, u32[]{:S(2)}, u32[]{:S(2)}) %collective-permute-start) | collective-permute-done | bytes 65568 | tf_op jit(solution)/shard_map/ppermute | solution.py:268
  16.0 2.5 %all-to-all-done = bf16[32,24,128]{2,1,0:T(8,128)(2,1)S(1)} async-done(((bf16[32,24,128]{2,1,0:T(8,128)(2,1)}), bf16[32,24,128]{2,1,0:T(8,128)(2,1)S(1)}, u32[]{:S(2)}, u32[]{:S(2)}) %all-to-all-start) | async-done | bytes 196640 | tf_op jit(solution)/shard_map/all_to_all | solution.py:384
  18.4 0.8 %shard_map.103 = (bf16[2,12,16,128]{3,2,1,0:T(8,128)(2,1)S(1)}, bf16[2,256,256]{2,1,0:T(8,128)(2,1)S(1)}, f32[2,4,16,128]{3,2,1,0:T(8,128)S(1)}) custom-call(bf16[256,512]{1,0:T(8,128)(2,1)S(1)} %get-tuple-element.18.after_ref.moves_ref, bf16[768,128]{1,0:T(8,128)(2,1)S(1)} %bitcast.4, f32[8,16,128]{2,1,0:T(8,128)S(1)} %get-tuple-element.20.refs_0_, ...), custom_call_target="tpu_custom_call" | custom-call | flops 536870912 | tf_op jit(solution)/shard_map/pallas_call | solution.py:395
  19.2 0.7 %collective-permute-start.1 = (bf16[2,12,16,128]{3,2,1,0:T(8,128)(2,1)S(1)}, bf16[2,12,16,128]{3,2,1,0:T(8,128)(2,1)S(1)}, u32[]{:S(2)}, u32[]{:S(2)}) collective-permute-start(bf16[2,12,16,128]{3,2,1,0:T(8,128)(2,1)S(1)} %get-tuple-element.24), channel_id=1, source_target_pairs={{0,1},{1,0},{2,3},{3,2},{4,5},{5,4},{6,7},{7,6},{8,9},{9,8},{10,11... | collective-permute-start | bytes 294920 | tf_op jit(solution)/shard_map/ppermute | solution.py:268
  19.9 0.7 %shard_map.104.refs_0_ = bf16[2,12,16,128]{3,2,1,0:T(8,128)(2,1)S(1)} custom-call(bf16[2,256,256]{2,1,0:T(8,128)(2,1)S(1)} %get-tuple-element.22.tables, f32[2,4,16,128]{3,2,1,0:T(8,128)S(1)} %get-tuple-element.23.owns, f32[8,16,128]{2,1,0:T(8,128)S(1)} %get-tuple-element.20.refs_0_, f32[8,16,128]{2,1,0:T(8,128)S(1)} %collective-permute-done.refs_1_), custom_call_target="tpu_custom_call" | custom-call | flops 536870912 | bytes 4000000 | tf_op jit(solution)/shard_map/pallas_call | solution.py:402
  20.6 0.2 collective-permute-done.1.refs_1_
  20.8 0.7 %shard_map.105 = f32[8,8,128]{2,1,0:T(8,128)S(1)} custom-call(s32[4,4]{1,0:T(4,128)S(4)} %get-tuple-element.15.cover_ref, s32[4]{0:T(128)S(4)} %get-tuple-element.16.count_ref, bf16[4,4,3,128,128]{4,3,2,1,0:T(8,128)(2,1)S(1)} %get-tuple-element.17.weight_ref, bf16[256,512]{1,0:T(8,128)(2,1)S(1)} %get-tuple-element.18.after_ref.moves_ref, ...), custom_call_target="tpu_custom_call" | custom-call | tf_op jit(solution)/shard_map/pallas_call | solution.py:414
  21.6 8.4 %all_to_all.16 = f32[8,8,128]{2,0,1:T(8,128)S(1)} all-to-all(f32[8,8,128]{2,0,1:T(8,128)S(1)} %bitcast.5), channel_id=1, replica_groups={{16,12,20,8,24,4,28,0},{17,13,21,9,25,5,29,1},{18,14,22,10,26,6,30,2},{..., dimensions={1} | all-to-all | bytes 65536 | tf_op jit(solution)/shard_map/all_to_all | solution.py:278
  30.0 0.7 %shard_map.106 = f32[12,512]{1,0:T(8,128)} custom-call(f32[8,8,128]{2,1,0:T(8,128)S(1)} %bitcast.6), custom_call_target="tpu_custom_call" | custom-call | tf_op jit(solution)/shard_map/pallas_call | solution.py:421
Async XLA Ops:
  2.2 16.2 %all-to-all-start = ((bf16[32,24,128]{2,1,0:T(8,128)(2,1)}), bf16[32,24,128]{2,1,0:T(8,128)(2,1)S(1)}, u32[]{:S(2)}, u32[]{:S(2)}) async-start(bf16[32,24,128]{2,1,0:T(8,128)(2,1)} %bitcast), calls=%async_computation | async-start | bytes 393216 | tf_op jit(solution)/shard_map/all_to_all | solution.py:384
  10.5 5.4 %collective-permute-start = (f32[8,16,128]{2,1,0:T(8,128)S(1)}, f32[8,16,128]{2,1,0:T(8,128)S(1)}, u32[]{:S(2)}, u32[]{:S(2)}) collective-permute-start(f32[8,16,128]{2,1,0:T(8,128)S(1)} %get-tuple-element.21), channel_id=1, source_target_pairs={{0,2},{1,3},{2,0},{3,1},{4,6},{5,7},{6,4},{7,5},{8,10},{9,11},{10,... | collective-permute-start | bytes 196616 | tf_op jit(solution)/shard_map/ppermute | solution.py:268
  19.2 1.6 %collective-permute-start.1 = (bf16[2,12,16,128]{3,2,1,0:T(8,128)(2,1)S(1)}, bf16[2,12,16,128]{3,2,1,0:T(8,128)(2,1)S(1)}, u32[]{:S(2)}, u32[]{:S(2)}) collective-permute-start(bf16[2,12,16,128]{3,2,1,0:T(8,128)(2,1)S(1)} %get-tuple-element.24), channel_id=1, source_target_pairs={{0,1},{1,0},{2,3},{3,2},{4,5},{5,4},{6,7},{7,6},{8,9},{9,8},{10,11... | collective-permute-start | bytes 294920 | tf_op jit(solution)/shard_map/ppermute | solution.py:268

commit v7 on v2

--- a/solution.py
+++ b/solution.py
@@ -31,11 +31,12 @@
     return result
 
 
-def lookup(table, index):
+def lookup(table, index, hot=None):
     results = []
     for at in range(0, index.shape[1], WIDTH):
         here = index[:, at : at + WIDTH]
-        found = jnp.dot(table, one_hot(here), preferred_element_type=jnp.float32)
+        made = one_hot(here) if hot is None else hot[:, at : at + WIDTH]
+        found = jnp.dot(table, made, preferred_element_type=jnp.float32)
         results.append(choose(found, here // DEPTH, ROWS))
     return jnp.concatenate(results, axis=1)
 
@@ -98,8 +99,8 @@
         copy.wait()
 
 
-def select_kernel(after_ref, list_hbm, near_hbm, x_hbm, y_hbm, *refs):
-    selected, (list_ref, near_ref, x_ref, y_ref, sems) = refs[:-5], refs[-5:]
+def select_kernel(twins, after_ref, list_hbm, near_hbm, x_hbm, y_hbm, *refs):
+    selected, hots, (list_ref, near_ref, x_ref, y_ref, sems) = refs[:twins], refs[twins:-5], refs[-5:]
     copies = copies_of((list_hbm, near_hbm, x_hbm, y_hbm), (list_ref, near_ref, x_ref, y_ref), sems)
     for copy in copies:
         copy.start()
@@ -118,6 +119,10 @@
             stencil_ref[at, 2 * near_count : 3 * near_count] = y_ref[:, columns]
             rest = (ROWS - 3 * near_count, LANES)
             stencil_ref[at, 3 * near_count :] = jnp.broadcast_to(block, rest).astype(jnp.float32)
+    for hot_ref in hots:
+        for at in range(hot_ref.shape[0]):
+            near = selected[0][cap + at, :near_count].astype(jnp.int32)
+            hot_ref[at] = one_hot(jnp.concatenate([near[j : j + 1] for j in range(near_count)], axis=1))
 
 
 def fetch_kernel(after_ref, map_hbm, *refs):
@@ -134,10 +139,10 @@
         copy.wait()
 
 
-def rebuild(near_count, table, stencil, own, shift):
+def rebuild(near_count, table, stencil, own, shift, hot=None):
     near = stencil[:near_count].astype(jnp.int32)
     index = jnp.concatenate([near[j : j + 1] for j in range(near_count)], axis=1)
-    found = lookup(table, index)
+    found = lookup(table, index, hot)
     upper = lower = own
     slope_x = slope_y = jnp.zeros_like(own)
     for j in range(near_count):
@@ -176,6 +181,7 @@
 
 def outer_kernel(twins, near_count, fields, after_ref, cells_ref, *refs):
     selected, refs = refs[:twins], refs[twins:]
+    hots, refs = refs[: twins - 1], refs[twins - 1 :]
     out_refs, (tables, owns) = refs[:-2], refs[-2:]
     cap = owns.shape[1]
     rows = message_rows(fields, twins)
@@ -190,7 +196,8 @@
                 owns[twin, at] = own
                 continue
             shift = twin * (fields - HALF)
-            results = rebuild(near_count, tables[twin], stencil_ref[at], own, shift)
+            hot = hots[0][at - cap] if hots and twin == 0 else None
+            results = rebuild(near_count, tables[twin], stencil_ref[at], own, shift, hot)
             for kind, result in enumerate(results):
                 out_refs[at // cap - 1][twin, at % cap * len(results) + kind] = result.astype(jnp.bfloat16)
 
@@ -350,9 +357,10 @@
     )(*stay(cell_map, atm_flux))
 
     stencil = shaped((aparts * cap, ROWS, LANES), jnp.float32)
+    hots = [shaped((cap, DEPTH, near_count * LANES), jnp.bfloat16)] * (twins - 1)
     selected = call(
-        select_kernel,
-        [stencil] * twins,
+        functools.partial(select_kernel, twins),
+        [stencil] * twins + hots,
         "ahhhh",
         [
             pltpu.SMEM(send_list.shape, send_list.dtype),
@@ -363,7 +371,8 @@
         ],
         moved=3_000_000,
     )(ordered, *stay(send_list, neighbours, coef_x, coef_y))
-    selected = [selected[0]] + [send(array, "local", 2) for array in selected[1:]]
+    hots = selected[twins:]
+    selected = [selected[0]] + [send(array, "local", 2) for array in selected[1:twins]]
 
     later = [cover, cover_count, weights]
     moves, high, cover, cover_count, weights = call(
@@ -396,9 +405,9 @@
     *outer, tables, owns = call(
         functools.partial(outer_kernel, twins, near_count, fields),
         [sent] * (aparts - 1) + [tables, owns],
-        "av" + "v" * twins,
+        "av" + "v" * twins + "v" * len(hots),
         flops=work * (aparts - 1),
-    )(moves, coupled, *selected)
+    )(moves, coupled, *selected, *hots)
     source = [send(array, "local", 1 + at) for at, array in enumerate(outer)]
     inner = call(
         functools.partial(inner_kernel, near_count, fields),

time: 31 us -> 31 us (level)
  transfers between devices with their start and end apart: 3 -> 3, of which waited for: 3 -> 3; matrix products, arithmetic and copies ran while one was open for 0% -> 0% of each run, Pallas kernels for 10% -> 11%
where the time goes in v7:
time: 31 us; the launch traced here: 30.6 us
  starting transfers between devices  9.79 us (32%)
  blocking collectives  8.44 us (27%)
  Pallas kernels  7.67 us (25%)
  waiting for transfers between devices  4.66 us (15%)
    all_to_all x1, blocking collectives, swap(): lax.all_to_all(pieces, axis, split_axis=1, concat_axis=1, axis_index_grou...  8.44 us
    all_to_all x1, starting transfers between devices, shards(): lax.all_to_all(ordered, everyone, split_axis=0, concat_axis=0, tiled=True)  7.3 us
    ppermute x2, starting transfers between devices, send(): lax.ppermute(array, axis, [(at, at ^ apart) for at in range(lax.axis_size...  2.49 us
    all_to_all x1, waiting for transfers between devices, shards(): lax.all_to_all(ordered, everyone, split_axis=0, concat_axis=0, tiled=True)  2.46 us
    ppermute x2, waiting for transfers between devices, send(): lax.ppermute(array, axis, [(at, at ^ apart) for at in range(lax.axis_size...  2.2 us
    pallas_call x1, Pallas kernels, shards(): call(functools.partial(order_kernel, twins), shaped(messages, jnp.bfloat1...  2.15 us
    pallas_call x1, Pallas kernels, shards(): call(fetch_kernel, [shaped((DEPTH, ocean_cells), jnp.bfloat16), shaped(oc...  1.46 us
    pallas_call x1, Pallas kernels, shards(): call(functools.partial(select_kernel, twins), [stencil] * twins + hots, '...  1.12 us
  transfers between devices with their start and end apart: 3, of which 3 were waited for; matrix products, arithmetic and copies ran while one was open for 0% of the time, Pallas kernels for 11%

profile of v7, /device:TPU:0, one launch (start us, length us, event | category | flops | bytes accessed | tf_op | source)
XLA Modules:
  0.0 30.6 jit_solution(16090557624931378581)
XLA Ops:
  0.0 2.1 %shard_map.100.after_ref = bf16[768,128]{1,0:T(8,128)(2,1)} custom-call(s32[1,4096]{1,0:T(1,128)} %map_hbm.2, bf16[12,4096]{1,0:T(8,128)(2,1)} %flux_hbm.1), custom_call_target="tpu_custom_call" | custom-call | tf_op jit(solution)/shard_map/pallas_call | solution.py:345
  2.2 7.3 %all-to-all-start = ((bf16[32,24,128]{2,1,0:T(8,128)(2,1)}), bf16[32,24,128]{2,1,0:T(8,128)(2,1)S(1)}, u32[]{:S(2)}, u32[]{:S(2)}) async-start(bf16[32,24,128]{2,1,0:T(8,128)(2,1)} %bitcast), calls=%async_computation | async-start | bytes 393216 | tf_op jit(solution)/shard_map/all_to_all | solution.py:394
  9.5 1.1 %shard_map.102 = (f32[8,16,128]{2,1,0:T(8,128)S(1)}, f32[8,16,128]{2,1,0:T(8,128)S(1)}, bf16[4,256,512]{2,1,0:T(8,128)(2,1)S(1)}) custom-call(bf16[768,128]{1,0:T(8,128)(2,1)} %shard_map.100.after_ref, s32[1,4,4]{2,1,0:T(4,128)} %list_hbm.1, s32[4,4096]{1,0:T(4,128)} %near_hbm.1, f32[4,4096]{1,0:T(4,128)} %x_hbm.1, f32[4,4096]{1,0:T(4,128)} %y_hbm.1), custom_call_target="tpu_custom_call" | custom-call | bytes 3000000 | tf_op jit(solution)/shard_map/pallas_call | solution.py:361
  10.6 1.8 %collective-permute-start = (f32[8,16,128]{2,1,0:T(8,128)S(1)}, f32[8,16,128]{2,1,0:T(8,128)S(1)}, u32[]{:S(2)}, u32[]{:S(2)}) collective-permute-start(f32[8,16,128]{2,1,0:T(8,128)S(1)} %get-tuple-element.22), channel_id=1, source_target_pairs={{0,2},{1,3},{2,0},{3,1},{4,6},{5,7},{6,4},{7,5},{8,10},{9,11},{10,... | collective-permute-start | bytes 196616 | tf_op jit(solution)/shard_map/ppermute | solution.py:276
  12.4 1.5 %shard_map.101 = (bf16[256,512]{1,0:T(8,128)(2,1)S(1)}, s32[1,512]{1,0:T(1,128)S(1)}, s32[4,4]{1,0:T(4,128)S(4)}, s32[4]{0:T(128)S(4)}, bf16[4,4,3,128,128]{4,3,2,1,0:T(8,128)(2,1)S(1)}) custom-call(bf16[768,128]{1,0:T(8,128)(2,1)} %shard_map.100.after_ref, s32[1,512]{1,0:T(1,128)} %map_hbm.3, s32[4,4]{1,0:T(4,128)} %refs_0_.1, s32[4]{0:T(128)} %refs_1_.1, ...), custom_call_target="tpu_custom_call" | custom-call | bytes 3000000 | tf_op jit(solution)/shard_map/pallas_call | solution.py:378
  13.9 2.0 %collective-permute-done.refs_1_ = f32[8,16,128]{2,1,0:T(8,128)S(1)} collective-permute-done((f32[8,16,128]{2,1,0:T(8,128)S(1)}, f32[8,16,128]{2,1,0:T(8,128)S(1)}, u32[]{:S(2)}, u32[]{:S(2)}) %collective-permute-start) | collective-permute-done | bytes 65568 | tf_op jit(solution)/shard_map/ppermute | solution.py:276
  15.9 2.5 %all-to-all-done = bf16[32,24,128]{2,1,0:T(8,128)(2,1)S(1)} async-done(((bf16[32,24,128]{2,1,0:T(8,128)(2,1)}), bf16[32,24,128]{2,1,0:T(8,128)(2,1)S(1)}, u32[]{:S(2)}, u32[]{:S(2)}) %all-to-all-start) | async-done | bytes 196640 | tf_op jit(solution)/shard_map/all_to_all | solution.py:394
  18.3 0.8 %shard_map.103 = (bf16[2,12,16,128]{3,2,1,0:T(8,128)(2,1)S(1)}, bf16[2,256,256]{2,1,0:T(8,128)(2,1)S(1)}, f32[2,4,16,128]{3,2,1,0:T(8,128)S(1)}) custom-call(bf16[256,512]{1,0:T(8,128)(2,1)S(1)} %get-tuple-element.19.after_ref.moves_ref, bf16[768,128]{1,0:T(8,128)(2,1)S(1)} %bitcast.4, f32[8,16,128]{2,1,0:T(8,128)S(1)} %get-tuple-element.21.refs_0_, ...), custom_call_target="tpu_custom_call" | custom-call | flops 536870912 | tf_op jit(solution)/shard_map/pallas_call | solution.py:405
  19.2 0.7 %collective-permute-start.1 = (bf16[2,12,16,128]{3,2,1,0:T(8,128)(2,1)S(1)}, bf16[2,12,16,128]{3,2,1,0:T(8,128)(2,1)S(1)}, u32[]{:S(2)}, u32[]{:S(2)}) collective-permute-start(bf16[2,12,16,128]{3,2,1,0:T(8,128)(2,1)S(1)} %get-tuple-element.26), channel_id=1, source_target_pairs={{0,1},{1,0},{2,3},{3,2},{4,5},{5,4},{6,7},{7,6},{8,9},{9,8},{10,11... | collective-permute-start | bytes 294920 | tf_op jit(solution)/shard_map/ppermute | solution.py:276
  19.8 0.7 %shard_map.104.refs_0_ = bf16[2,12,16,128]{3,2,1,0:T(8,128)(2,1)S(1)} custom-call(bf16[2,256,256]{2,1,0:T(8,128)(2,1)S(1)} %get-tuple-element.24.tables, f32[2,4,16,128]{3,2,1,0:T(8,128)S(1)} %get-tuple-element.25.owns, f32[8,16,128]{2,1,0:T(8,128)S(1)} %get-tuple-element.21.refs_0_, f32[8,16,128]{2,1,0:T(8,128)S(1)} %collective-permute-done.refs_1_), custom_call_target="tpu_custom_call" | custom-call | flops 536870912 | bytes 4000000 | tf_op jit(solution)/shard_map/pallas_call | solution.py:412
  20.6 0.2 collective-permute-done.1.refs_1_
  20.8 0.7 %shard_map.105 = f32[8,8,128]{2,1,0:T(8,128)S(1)} custom-call(s32[4,4]{1,0:T(4,128)S(4)} %get-tuple-element.16.cover_ref, s32[4]{0:T(128)S(4)} %get-tuple-element.17.count_ref, bf16[4,4,3,128,128]{4,3,2,1,0:T(8,128)(2,1)S(1)} %get-tuple-element.18.weight_ref, bf16[256,512]{1,0:T(8,128)(2,1)S(1)} %get-tuple-element.19.after_ref.moves_ref, ...), custom_call_target="tpu_custom_call" | custom-call | tf_op jit(solution)/shard_map/pallas_call | solution.py:424
  21.5 8.4 %all_to_all.16 = f32[8,8,128]{2,0,1:T(8,128)S(1)} all-to-all(f32[8,8,128]{2,0,1:T(8,128)S(1)} %bitcast.5), channel_id=1, replica_groups={{16,12,20,8,24,4,28,0},{17,13,21,9,25,5,29,1},{18,14,22,10,26,6,30,2},{..., dimensions={1} | all-to-all | bytes 65536 | tf_op jit(solution)/shard_map/all_to_all | solution.py:286
  29.9 0.7 %shard_map.106 = f32[12,512]{1,0:T(8,128)} custom-call(f32[8,8,128]{2,1,0:T(8,128)S(1)} %bitcast.6), custom_call_target="tpu_custom_call" | custom-call | tf_op jit(solution)/shard_map/pallas_call | solution.py:432
Async XLA Ops:
  2.2 16.2 %all-to-all-start = ((bf16[32,24,128]{2,1,0:T(8,128)(2,1)}), bf16[32,24,128]{2,1,0:T(8,128)(2,1)S(1)}, u32[]{:S(2)}, u32[]{:S(2)}) async-start(bf16[32,24,128]{2,1,0:T(8,128)(2,1)} %bitcast), calls=%async_computation | async-start | bytes 393216 | tf_op jit(solution)/shard_map/all_to_all | solution.py:394
  10.6 5.3 %collective-permute-start = (f32[8,16,128]{2,1,0:T(8,128)S(1)}, f32[8,16,128]{2,1,0:T(8,128)S(1)}, u32[]{:S(2)}, u32[]{:S(2)}) collective-permute-start(f32[8,16,128]{2,1,0:T(8,128)S(1)} %get-tuple-element.22), channel_id=1, source_target_pairs={{0,2},{1,3},{2,0},{3,1},{4,6},{5,7},{6,4},{7,5},{8,10},{9,11},{10,... | collective-permute-start | bytes 196616 | tf_op jit(solution)/shard_map/ppermute | solution.py:276
  19.2 1.6 %collective-permute-start.1 = (bf16[2,12,16,128]{3,2,1,0:T(8,128)(2,1)S(1)}, bf16[2,12,16,128]{3,2,1,0:T(8,128)(2,1)S(1)}, u32[]{:S(2)}, u32[]{:S(2)}) collective-permute-start(bf16[2,12,16,128]{3,2,1,0:T(8,128)(2,1)S(1)} %get-tuple-element.26), channel_id=1, source_target_pairs={{0,1},{1,0},{2,3},{3,2},{4,5},{5,4},{6,7},{7,6},{8,9},{9,8},{10,11... | collective-permute-start | bytes 294920 | tf_op jit(solution)/shard_map/ppermute | solution.py:276

commit v8 on v2

--- a/solution.py
+++ b/solution.py
@@ -35,8 +35,8 @@
     results = []
     for at in range(0, index.shape[1], WIDTH):
         here = index[:, at : at + WIDTH]
-        found = jnp.dot(table, one_hot(here), preferred_element_type=jnp.float32)
-        results.append(choose(found, here // DEPTH, ROWS))
+        found = jnp.dot(table, one_hot(here), preferred_element_type=jnp.float32).astype(jnp.bfloat16)
+        results.append(choose(found, (here // DEPTH).astype(jnp.int16), ROWS).astype(jnp.float32))
     return jnp.concatenate(results, axis=1)
 
 

time: 31 us -> 31 us (level)
  no operation moved by 1% of the time
where the time goes in v8:
time: 31 us; the launch traced here: 30.6 us
  starting transfers between devices  9.79 us (32%)
  blocking collectives  8.45 us (27%)
  Pallas kernels  7.54 us (24%)
  waiting for transfers between devices  4.8 us (15%)
    all_to_all x1, blocking collectives, swap(): lax.all_to_all(pieces, axis, split_axis=1, concat_axis=1, axis_index_grou...  8.45 us
    all_to_all x1, starting transfers between devices, shards(): lax.all_to_all(ordered, everyone, split_axis=0, concat_axis=0, tiled=True)  7.3 us
    ppermute x2, starting transfers between devices, send(): lax.ppermute(array, axis, [(at, at ^ apart) for at in range(lax.axis_size...  2.49 us
    all_to_all x1, waiting for transfers between devices, shards(): lax.all_to_all(ordered, everyone, split_axis=0, concat_axis=0, tiled=True)  2.47 us
    ppermute x2, waiting for transfers between devices, send(): lax.ppermute(array, axis, [(at, at ^ apart) for at in range(lax.axis_size...  2.33 us
    pallas_call x1, Pallas kernels, shards(): call(functools.partial(order_kernel, twins), shaped(messages, jnp.bfloat1...  2.15 us
    pallas_call x1, Pallas kernels, shards(): call(fetch_kernel, [shaped((DEPTH, ocean_cells), jnp.bfloat16), shaped(oc...  1.46 us
    pallas_call x1, Pallas kernels, shards(): call(select_kernel, [stencil] * twins, 'ahhhh', [pltpu.SMEM(send_list.sha...  0.98 us
  transfers between devices with their start and end apart: 3, of which 3 were waited for; matrix products, arithmetic and copies ran while one was open for 0% of the time, Pallas kernels for 10%

profile of v8, /device:TPU:0, one launch (start us, length us, event | category | flops | bytes accessed | tf_op | source)
XLA Modules:
  0.0 30.6 jit_solution(15982999724478767754)
XLA Ops:
  0.0 2.1 %shard_map.100.after_ref = bf16[768,128]{1,0:T(8,128)(2,1)} custom-call(s32[1,4096]{1,0:T(1,128)} %map_hbm.2, bf16[12,4096]{1,0:T(8,128)(2,1)} %flux_hbm.1), custom_call_target="tpu_custom_call" | custom-call | tf_op jit(solution)/shard_map/pallas_call | solution.py:338
  2.2 7.3 %all-to-all-start = ((bf16[32,24,128]{2,1,0:T(8,128)(2,1)}), bf16[32,24,128]{2,1,0:T(8,128)(2,1)S(1)}, u32[]{:S(2)}, u32[]{:S(2)}) async-start(bf16[32,24,128]{2,1,0:T(8,128)(2,1)} %bitcast), calls=%async_computation | async-start | bytes 393216 | tf_op jit(solution)/shard_map/all_to_all | solution.py:385
  9.5 1.0 %shard_map.102 = (f32[8,16,128]{2,1,0:T(8,128)S(1)}, f32[8,16,128]{2,1,0:T(8,128)S(1)}) custom-call(bf16[768,128]{1,0:T(8,128)(2,1)} %shard_map.100.after_ref, s32[1,4,4]{2,1,0:T(4,128)} %list_hbm.1, s32[4,4096]{1,0:T(4,128)} %near_hbm.1, f32[4,4096]{1,0:T(4,128)} %x_hbm.1, f32[4,4096]{1,0:T(4,128)} %y_hbm.1), custom_call_target="tpu_custom_call" | custom-call | bytes 3000000 | tf_op jit(solution)/shard_map/pallas_call | solution.py:353
  10.4 1.8 %collective-permute-start = (f32[8,16,128]{2,1,0:T(8,128)S(1)}, f32[8,16,128]{2,1,0:T(8,128)S(1)}, u32[]{:S(2)}, u32[]{:S(2)}) collective-permute-start(f32[8,16,128]{2,1,0:T(8,128)S(1)} %get-tuple-element.21), channel_id=1, source_target_pairs={{0,2},{1,3},{2,0},{3,1},{4,6},{5,7},{6,4},{7,5},{8,10},{9,11},{10,... | collective-permute-start | bytes 196616 | tf_op jit(solution)/shard_map/ppermute | solution.py:269
  12.3 1.5 %shard_map.101 = (bf16[256,512]{1,0:T(8,128)(2,1)S(1)}, s32[1,512]{1,0:T(1,128)S(1)}, s32[4,4]{1,0:T(4,128)S(4)}, s32[4]{0:T(128)S(4)}, bf16[4,4,3,128,128]{4,3,2,1,0:T(8,128)(2,1)S(1)}) custom-call(bf16[768,128]{1,0:T(8,128)(2,1)} %shard_map.100.after_ref, s32[1,512]{1,0:T(1,128)} %map_hbm.3, s32[4,4]{1,0:T(4,128)} %refs_0_.1, s32[4]{0:T(128)} %refs_1_.1, ...), custom_call_target="tpu_custom_call" | custom-call | bytes 3000000 | tf_op jit(solution)/shard_map/pallas_call | solution.py:369
  13.7 2.1 %collective-permute-done.refs_1_ = f32[8,16,128]{2,1,0:T(8,128)S(1)} collective-permute-done((f32[8,16,128]{2,1,0:T(8,128)S(1)}, f32[8,16,128]{2,1,0:T(8,128)S(1)}, u32[]{:S(2)}, u32[]{:S(2)}) %collective-permute-start) | collective-permute-done | bytes 65568 | tf_op jit(solution)/shard_map/ppermute | solution.py:269
  15.9 2.5 %all-to-all-done = bf16[32,24,128]{2,1,0:T(8,128)(2,1)S(1)} async-done(((bf16[32,24,128]{2,1,0:T(8,128)(2,1)}), bf16[32,24,128]{2,1,0:T(8,128)(2,1)S(1)}, u32[]{:S(2)}, u32[]{:S(2)}) %all-to-all-start) | async-done | bytes 196640 | tf_op jit(solution)/shard_map/all_to_all | solution.py:385
  18.3 0.8 %shard_map.103 = (bf16[2,12,16,128]{3,2,1,0:T(8,128)(2,1)S(1)}, bf16[2,256,256]{2,1,0:T(8,128)(2,1)S(1)}, f32[2,4,16,128]{3,2,1,0:T(8,128)S(1)}) custom-call(bf16[256,512]{1,0:T(8,128)(2,1)S(1)} %get-tuple-element.18.after_ref.moves_ref, bf16[768,128]{1,0:T(8,128)(2,1)S(1)} %bitcast.4, f32[8,16,128]{2,1,0:T(8,128)S(1)} %get-tuple-element.20.refs_0_, ...), custom_call_target="tpu_custom_call" | custom-call | flops 536870912 | tf_op jit(solution)/shard_map/pallas_call | solution.py:396
  19.2 0.7 %collective-permute-start.1 = (bf16[2,12,16,128]{3,2,1,0:T(8,128)(2,1)S(1)}, bf16[2,12,16,128]{3,2,1,0:T(8,128)(2,1)S(1)}, u32[]{:S(2)}, u32[]{:S(2)}) collective-permute-start(bf16[2,12,16,128]{3,2,1,0:T(8,128)(2,1)S(1)} %get-tuple-element.24), channel_id=1, source_target_pairs={{0,1},{1,0},{2,3},{3,2},{4,5},{5,4},{6,7},{7,6},{8,9},{9,8},{10,11... | collective-permute-start | bytes 294920 | tf_op jit(solution)/shard_map/ppermute | solution.py:269
  19.8 0.7 %shard_map.104.refs_0_ = bf16[2,12,16,128]{3,2,1,0:T(8,128)(2,1)S(1)} custom-call(bf16[2,256,256]{2,1,0:T(8,128)(2,1)S(1)} %get-tuple-element.22.tables, f32[2,4,16,128]{3,2,1,0:T(8,128)S(1)} %get-tuple-element.23.owns, f32[8,16,128]{2,1,0:T(8,128)S(1)} %get-tuple-element.20.refs_0_, f32[8,16,128]{2,1,0:T(8,128)S(1)} %collective-permute-done.refs_1_), custom_call_target="tpu_custom_call" | custom-call | flops 536870912 | bytes 4000000 | tf_op jit(solution)/shard_map/pallas_call | solution.py:403
  20.6 0.2 collective-permute-done.1.refs_1_
  20.8 0.7 %shard_map.105 = f32[8,8,128]{2,1,0:T(8,128)S(1)} custom-call(s32[4,4]{1,0:T(4,128)S(4)} %get-tuple-element.15.cover_ref, s32[4]{0:T(128)S(4)} %get-tuple-element.16.count_ref, bf16[4,4,3,128,128]{4,3,2,1,0:T(8,128)(2,1)S(1)} %get-tuple-element.17.weight_ref, bf16[256,512]{1,0:T(8,128)(2,1)S(1)} %get-tuple-element.18.after_ref.moves_ref, ...), custom_call_target="tpu_custom_call" | custom-call | tf_op jit(solution)/shard_map/pallas_call | solution.py:415
  21.5 8.5 %all_to_all.16 = f32[8,8,128]{2,0,1:T(8,128)S(1)} all-to-all(f32[8,8,128]{2,0,1:T(8,128)S(1)} %bitcast.5), channel_id=1, replica_groups={{16,12,20,8,24,4,28,0},{17,13,21,9,25,5,29,1},{18,14,22,10,26,6,30,2},{..., dimensions={1} | all-to-all | bytes 65536 | tf_op jit(solution)/shard_map/all_to_all | solution.py:279
  29.9 0.7 %shard_map.106 = f32[12,512]{1,0:T(8,128)} custom-call(f32[8,8,128]{2,1,0:T(8,128)S(1)} %bitcast.6), custom_call_target="tpu_custom_call" | custom-call | tf_op jit(solution)/shard_map/pallas_call | solution.py:423
Async XLA Ops:
  2.2 16.2 %all-to-all-start = ((bf16[32,24,128]{2,1,0:T(8,128)(2,1)}), bf16[32,24,128]{2,1,0:T(8,128)(2,1)S(1)}, u32[]{:S(2)}, u32[]{:S(2)}) async-start(bf16[32,24,128]{2,1,0:T(8,128)(2,1)} %bitcast), calls=%async_computation | async-start | bytes 393216 | tf_op jit(solution)/shard_map/all_to_all | solution.py:385
  10.4 5.4 %collective-permute-start = (f32[8,16,128]{2,1,0:T(8,128)S(1)}, f32[8,16,128]{2,1,0:T(8,128)S(1)}, u32[]{:S(2)}, u32[]{:S(2)}) collective-permute-start(f32[8,16,128]{2,1,0:T(8,128)S(1)} %get-tuple-element.21), channel_id=1, source_target_pairs={{0,2},{1,3},{2,0},{3,1},{4,6},{5,7},{6,4},{7,5},{8,10},{9,11},{10,... | collective-permute-start | bytes 196616 | tf_op jit(solution)/shard_map/ppermute | solution.py:269
  19.2 1.6 %collective-permute-start.1 = (bf16[2,12,16,128]{3,2,1,0:T(8,128)(2,1)S(1)}, bf16[2,12,16,128]{3,2,1,0:T(8,128)(2,1)S(1)}, u32[]{:S(2)}, u32[]{:S(2)}) collective-permute-start(bf16[2,12,16,128]{3,2,1,0:T(8,128)(2,1)S(1)} %get-tuple-element.24), channel_id=1, source_target_pairs={{0,1},{1,0},{2,3},{3,2},{4,5},{5,4},{6,7},{7,6},{8,9},{9,8},{10,11... | collective-permute-start | bytes 294920 | tf_op jit(solution)/shard_map/ppermute | solution.py:269

commit v9 on v2

--- a/solution.py
+++ b/solution.py
@@ -62,6 +62,10 @@
 
 def message_rows(fields, twins):
     return 2 * fields if twins == 2 else ROWS
+
+
+def place_of(device, twins):
+    return device ^ 1 if twins == 2 else device
 
 
 def order_kernel(twins, map_hbm, flux_hbm, out_hbm, map_ref, flux_ref, out_ref, table, sems):
@@ -89,7 +93,7 @@
                 jnp.concatenate([pieces[at][:fields], pieces[at ^ 2][:fields]], axis=0) for at in range(len(pieces))
             ]
         for at, piece in enumerate(pieces):
-            first = (step * len(pieces) + at) * rows
+            first = place_of(step * len(pieces) + at, twins) * rows
             out_ref[first : first + rows] = piece.astype(jnp.bfloat16)
         span = pl.ds(step * len(pieces) * rows, len(pieces) * rows)
         written.append(pltpu.make_async_copy(out_ref.at[span], out_hbm.at[span], sems.at[5 + step]))
@@ -182,7 +186,7 @@
     for twin in range(twins):
         for block in range(tables.shape[1] // ROWS * PER_ROW):
             part, column = block // PER_ROW, block % PER_ROW * LANES
-            first = block * rows + HALF * twin
+            first = place_of(block, twins) * rows + HALF * twin
             tables[twin, part * ROWS : (part + 1) * ROWS, column : column + LANES] = cells_ref[first : first + ROWS]
     for twin, stencil_ref in enumerate(selected):
         for at, own in enumerate(own_cells(near_count, tables[twin], stencil_ref)):
@@ -382,7 +386,10 @@
     )(ordered, *stay(ocean_map, *later))
 
     if piece == LANES:
-        coupled = lax.all_to_all(ordered, everyone, split_axis=0, concat_axis=0, tiled=True)
+        listed = [place_of(device, twins) for device in range(devices)]
+        coupled = lax.all_to_all(
+            ordered, everyone, split_axis=0, concat_axis=0, axis_index_groups=[listed], tiled=True
+        )
     else:
         outgoing = ordered.reshape(blocks, rows, LANES)[:, :fields].transpose(1, 0, 2).reshape(fields, devices, piece)
         coupled = lax.all_to_all(outgoing, everyone, split_axis=1, concat_axis=1, tiled=True)

time: 31 us -> 30.9 us (level)
  starting transfers between devices: 9.79 us -> 9.2 us
  waiting for transfers between devices: 4.8 us -> 5.38 us
    ppermute x2, starting transfers between devices: 2.49 us -> 1.9 us  [send(): lax.ppermute(array, axis, [(at, at ^ apart) for at in range(lax.axis_size...]
where the time goes in v9:
time: 30.9 us; the launch traced here: 30.5 us
  starting transfers between devices  9.2 us (30%)
  blocking collectives  8.34 us (27%)
  Pallas kernels  7.54 us (24%)
  waiting for transfers between devices  5.38 us (17%)
    all_to_all x1, blocking collectives, swap(): lax.all_to_all(pieces, axis, split_axis=1, concat_axis=1, axis_index_grou...  8.34 us
    all_to_all x1, starting transfers between devices, shards(): lax.all_to_all(ordered, everyone, split_axis=0, concat_axis=0, axis_index...  7.3 us
    all_to_all x1, waiting for transfers between devices, shards(): lax.all_to_all(ordered, everyone, split_axis=0, concat_axis=0, axis_index...  2.77 us
    ppermute x2, waiting for transfers between devices, send(): lax.ppermute(array, axis, [(at, at ^ apart) for at in range(lax.axis_size...  2.61 us
    pallas_call x1, Pallas kernels, shards(): call(functools.partial(order_kernel, twins), shaped(messages, jnp.bfloat1...  2.15 us
    ppermute x2, starting transfers between devices, send(): lax.ppermute(array, axis, [(at, at ^ apart) for at in range(lax.axis_size...  1.9 us
    pallas_call x1, Pallas kernels, shards(): call(fetch_kernel, [shaped((DEPTH, ocean_cells), jnp.bfloat16), shaped(oc...  1.46 us
    pallas_call x1, Pallas kernels, shards(): call(select_kernel, [stencil] * twins, 'ahhhh', [pltpu.SMEM(send_list.sha...  0.98 us
  transfers between devices with their start and end apart: 3, of which 3 were waited for; matrix products, arithmetic and copies ran while one was open for 0% of the time, Pallas kernels for 10%

profile of v9, /device:TPU:0, one launch (start us, length us, event | category | flops | bytes accessed | tf_op | source)
XLA Modules:
  0.0 30.5 jit_solution(2675994100612638762)
XLA Ops:
  0.0 2.1 %shard_map.100.after_ref = bf16[768,128]{1,0:T(8,128)(2,1)} custom-call(s32[1,4096]{1,0:T(1,128)} %map_hbm.2, bf16[12,4096]{1,0:T(8,128)(2,1)} %flux_hbm.1), custom_call_target="tpu_custom_call" | custom-call | tf_op jit(solution)/shard_map/pallas_call | solution.py:342
  2.2 7.3 %all-to-all-start = ((bf16[32,24,128]{2,1,0:T(8,128)(2,1)}), bf16[32,24,128]{2,1,0:T(8,128)(2,1)S(1)}, u32[]{:S(2)}, u32[]{:S(2)}) async-start(bf16[32,24,128]{2,1,0:T(8,128)(2,1)} %bitcast), calls=%async_computation | async-start | bytes 393216 | tf_op jit(solution)/shard_map/all_to_all | solution.py:390
  9.5 1.0 %shard_map.102 = (f32[8,16,128]{2,1,0:T(8,128)S(1)}, f32[8,16,128]{2,1,0:T(8,128)S(1)}) custom-call(bf16[768,128]{1,0:T(8,128)(2,1)} %shard_map.100.after_ref, s32[1,4,4]{2,1,0:T(4,128)} %list_hbm.1, s32[4,4096]{1,0:T(4,128)} %near_hbm.1, f32[4,4096]{1,0:T(4,128)} %x_hbm.1, f32[4,4096]{1,0:T(4,128)} %y_hbm.1), custom_call_target="tpu_custom_call" | custom-call | bytes 3000000 | tf_op jit(solution)/shard_map/pallas_call | solution.py:357
  10.5 1.8 %collective-permute-start = (f32[8,16,128]{2,1,0:T(8,128)S(1)}, f32[8,16,128]{2,1,0:T(8,128)S(1)}, u32[]{:S(2)}, u32[]{:S(2)}) collective-permute-start(f32[8,16,128]{2,1,0:T(8,128)S(1)} %get-tuple-element.21), channel_id=1, source_target_pairs={{0,2},{1,3},{2,0},{3,1},{4,6},{5,7},{6,4},{7,5},{8,10},{9,11},{10,... | collective-permute-start | bytes 196616 | tf_op jit(solution)/shard_map/ppermute | solution.py:273
  12.3 1.5 %shard_map.101 = (bf16[256,512]{1,0:T(8,128)(2,1)S(1)}, s32[1,512]{1,0:T(1,128)S(1)}, s32[4,4]{1,0:T(4,128)S(4)}, s32[4]{0:T(128)S(4)}, bf16[4,4,3,128,128]{4,3,2,1,0:T(8,128)(2,1)S(1)}) custom-call(bf16[768,128]{1,0:T(8,128)(2,1)} %shard_map.100.after_ref, s32[1,512]{1,0:T(1,128)} %map_hbm.3, s32[4,4]{1,0:T(4,128)} %refs_0_.1, s32[4]{0:T(128)} %refs_1_.1, ...), custom_call_target="tpu_custom_call" | custom-call | bytes 3000000 | tf_op jit(solution)/shard_map/pallas_call | solution.py:373
  13.8 2.1 %collective-permute-done.refs_1_ = f32[8,16,128]{2,1,0:T(8,128)S(1)} collective-permute-done((f32[8,16,128]{2,1,0:T(8,128)S(1)}, f32[8,16,128]{2,1,0:T(8,128)S(1)}, u32[]{:S(2)}, u32[]{:S(2)}) %collective-permute-start) | collective-permute-done | bytes 65568 | tf_op jit(solution)/shard_map/ppermute | solution.py:273
  15.8 2.8 %all-to-all-done = bf16[32,24,128]{2,1,0:T(8,128)(2,1)S(1)} async-done(((bf16[32,24,128]{2,1,0:T(8,128)(2,1)}), bf16[32,24,128]{2,1,0:T(8,128)(2,1)S(1)}, u32[]{:S(2)}, u32[]{:S(2)}) %all-to-all-start) | async-done | bytes 196640 | tf_op jit(solution)/shard_map/all_to_all | solution.py:390
  18.6 0.8 %shard_map.103 = (bf16[2,12,16,128]{3,2,1,0:T(8,128)(2,1)S(1)}, bf16[2,256,256]{2,1,0:T(8,128)(2,1)S(1)}, f32[2,4,16,128]{3,2,1,0:T(8,128)S(1)}) custom-call(bf16[256,512]{1,0:T(8,128)(2,1)S(1)} %get-tuple-element.18.after_ref.moves_ref, bf16[768,128]{1,0:T(8,128)(2,1)S(1)} %bitcast.4, f32[8,16,128]{2,1,0:T(8,128)S(1)} %get-tuple-element.20.refs_0_, ...), custom_call_target="tpu_custom_call" | custom-call | flops 536870912 | tf_op jit(solution)/shard_map/pallas_call | solution.py:403
  19.4 0.1 collective-permute-start.1
  19.5 0.7 %shard_map.104.refs_0_ = bf16[2,12,16,128]{3,2,1,0:T(8,128)(2,1)S(1)} custom-call(bf16[2,256,256]{2,1,0:T(8,128)(2,1)S(1)} %get-tuple-element.22.tables, f32[2,4,16,128]{3,2,1,0:T(8,128)S(1)} %get-tuple-element.23.owns, f32[8,16,128]{2,1,0:T(8,128)S(1)} %get-tuple-element.20.refs_0_, f32[8,16,128]{2,1,0:T(8,128)S(1)} %collective-permute-done.refs_1_), custom_call_target="tpu_custom_call" | custom-call | flops 536870912 | bytes 4000000 | tf_op jit(solution)/shard_map/pallas_call | solution.py:410
  20.2 0.5 %collective-permute-done.1.refs_1_ = bf16[2,12,16,128]{3,2,1,0:T(8,128)(2,1)S(1)} collective-permute-done((bf16[2,12,16,128]{3,2,1,0:T(8,128)(2,1)S(1)}, bf16[2,12,16,128]{3,2,1,0:T(8,128)(2,1)S(1)}, u32[]{:S(2)}, u32[]{:S(2)}) %collective-permute-start.1) | collective-permute-done | bytes 98336 | tf_op jit(solution)/shard_map/ppermute | solution.py:273
  20.8 0.7 %shard_map.105 = f32[8,8,128]{2,1,0:T(8,128)S(1)} custom-call(s32[4,4]{1,0:T(4,128)S(4)} %get-tuple-element.15.cover_ref, s32[4]{0:T(128)S(4)} %get-tuple-element.16.count_ref, bf16[4,4,3,128,128]{4,3,2,1,0:T(8,128)(2,1)S(1)} %get-tuple-element.17.weight_ref, bf16[256,512]{1,0:T(8,128)(2,1)S(1)} %get-tuple-element.18.after_ref.moves_ref, ...), custom_call_target="tpu_custom_call" | custom-call | tf_op jit(solution)/shard_map/pallas_call | solution.py:422
  21.5 8.3 %all_to_all.16 = f32[8,8,128]{2,0,1:T(8,128)S(1)} all-to-all(f32[8,8,128]{2,0,1:T(8,128)S(1)} %bitcast.5), channel_id=1, replica_groups={{16,12,20,8,24,4,28,0},{17,13,21,9,25,5,29,1},{18,14,22,10,26,6,30,2},{..., dimensions={1} | all-to-all | bytes 65536 | tf_op jit(solution)/shard_map/all_to_all | solution.py:283
  29.8 0.7 %shard_map.106 = f32[12,512]{1,0:T(8,128)} custom-call(f32[8,8,128]{2,1,0:T(8,128)S(1)} %bitcast.6), custom_call_target="tpu_custom_call" | custom-call | tf_op jit(solution)/shard_map/pallas_call | solution.py:430
Async XLA Ops:
  2.2 16.4 %all-to-all-start = ((bf16[32,24,128]{2,1,0:T(8,128)(2,1)}), bf16[32,24,128]{2,1,0:T(8,128)(2,1)S(1)}, u32[]{:S(2)}, u32[]{:S(2)}) async-start(bf16[32,24,128]{2,1,0:T(8,128)(2,1)} %bitcast), calls=%async_computation | async-start | bytes 393216 | tf_op jit(solution)/shard_map/all_to_all | solution.py:390
  10.5 5.4 %collective-permute-start = (f32[8,16,128]{2,1,0:T(8,128)S(1)}, f32[8,16,128]{2,1,0:T(8,128)S(1)}, u32[]{:S(2)}, u32[]{:S(2)}) collective-permute-start(f32[8,16,128]{2,1,0:T(8,128)S(1)} %get-tuple-element.21), channel_id=1, source_target_pairs={{0,2},{1,3},{2,0},{3,1},{4,6},{5,7},{6,4},{7,5},{8,10},{9,11},{10,... | collective-permute-start | bytes 196616 | tf_op jit(solution)/shard_map/ppermute | solution.py:273
  19.4 1.4 %collective-permute-start.1 = (bf16[2,12,16,128]{3,2,1,0:T(8,128)(2,1)S(1)}, bf16[2,12,16,128]{3,2,1,0:T(8,128)(2,1)S(1)}, u32[]{:S(2)}, u32[]{:S(2)}) collective-permute-start(bf16[2,12,16,128]{3,2,1,0:T(8,128)(2,1)S(1)} %get-tuple-element.24), channel_id=1, source_target_pairs={{0,1},{1,0},{2,3},{3,2},{4,5},{5,4},{6,7},{7,6},{8,9},{9,8},{10,11... | collective-permute-start | bytes 294920 | tf_op jit(solution)/shard_map/ppermute | solution.py:273

commit v10 on v9

--- a/solution.py
+++ b/solution.py
@@ -65,7 +65,7 @@
 
 
 def place_of(device, twins):
-    return device ^ 1 if twins == 2 else device
+    return device ^ 4 if twins == 2 else device
 
 
 def order_kernel(twins, map_hbm, flux_hbm, out_hbm, map_ref, flux_ref, out_ref, table, sems):
@@ -95,7 +95,7 @@
         for at, piece in enumerate(pieces):
             first = place_of(step * len(pieces) + at, twins) * rows
             out_ref[first : first + rows] = piece.astype(jnp.bfloat16)
-        span = pl.ds(step * len(pieces) * rows, len(pieces) * rows)
+        span = pl.ds(place_of(step * len(pieces), twins) * rows, len(pieces) * rows)
         written.append(pltpu.make_async_copy(out_ref.at[span], out_hbm.at[span], sems.at[5 + step]))
         written[-1].start()
     for copy in written:

time: 30.9 us -> 31 us (level)
  no operation moved by 1% of the time
where the time goes in v10:
time: 31 us; the launch traced here: 30.6 us
  starting transfers between devices  9.2 us (30%)
  blocking collectives  8.32 us (27%)
  Pallas kernels  7.53 us (24%)
  waiting for transfers between devices  5.54 us (18%)
    all_to_all x1, blocking collectives, swap(): lax.all_to_all(pieces, axis, split_axis=1, concat_axis=1, axis_index_grou...  8.32 us
    all_to_all x1, starting transfers between devices, shards(): lax.all_to_all(ordered, everyone, split_axis=0, concat_axis=0, axis_index...  7.3 us
    all_to_all x1, waiting for transfers between devices, shards(): lax.all_to_all(ordered, everyone, split_axis=0, concat_axis=0, axis_index...  2.99 us
    ppermute x2, waiting for transfers between devices, send(): lax.ppermute(array, axis, [(at, at ^ apart) for at in range(lax.axis_size...  2.54 us
    pallas_call x1, Pallas kernels, shards(): call(functools.partial(order_kernel, twins), shaped(messages, jnp.bfloat1...  2.14 us
    ppermute x2, starting transfers between devices, send(): lax.ppermute(array, axis, [(at, at ^ apart) for at in range(lax.axis_size...  1.9 us
    pallas_call x1, Pallas kernels, shards(): call(fetch_kernel, [shaped((DEPTH, ocean_cells), jnp.bfloat16), shaped(oc...  1.46 us
    pallas_call x1, Pallas kernels, shards(): call(select_kernel, [stencil] * twins, 'ahhhh', [pltpu.SMEM(send_list.sha...  0.98 us
  transfers between devices with their start and end apart: 3, of which 3 were waited for; matrix products, arithmetic and copies ran while one was open for 0% of the time, Pallas kernels for 10%

profile of v10, /device:TPU:0, one launch (start us, length us, event | category | flops | bytes accessed | tf_op | source)
XLA Modules:
  0.0 30.6 jit_solution(5451694241638311270)
XLA Ops:
  0.0 2.1 %shard_map.100.after_ref = bf16[768,128]{1,0:T(8,128)(2,1)} custom-call(s32[1,4096]{1,0:T(1,128)} %map_hbm.2, bf16[12,4096]{1,0:T(8,128)(2,1)} %flux_hbm.1), custom_call_target="tpu_custom_call" | custom-call | tf_op jit(solution)/shard_map/pallas_call | solution.py:342
  2.1 7.3 %all-to-all-start = ((bf16[32,24,128]{2,1,0:T(8,128)(2,1)}), bf16[32,24,128]{2,1,0:T(8,128)(2,1)S(1)}, u32[]{:S(2)}, u32[]{:S(2)}) async-start(bf16[32,24,128]{2,1,0:T(8,128)(2,1)} %bitcast), calls=%async_computation | async-start | bytes 393216 | tf_op jit(solution)/shard_map/all_to_all | solution.py:390
  9.5 1.0 %shard_map.102 = (f32[8,16,128]{2,1,0:T(8,128)S(1)}, f32[8,16,128]{2,1,0:T(8,128)S(1)}) custom-call(bf16[768,128]{1,0:T(8,128)(2,1)} %shard_map.100.after_ref, s32[1,4,4]{2,1,0:T(4,128)} %list_hbm.1, s32[4,4096]{1,0:T(4,128)} %near_hbm.1, f32[4,4096]{1,0:T(4,128)} %x_hbm.1, f32[4,4096]{1,0:T(4,128)} %y_hbm.1), custom_call_target="tpu_custom_call" | custom-call | bytes 3000000 | tf_op jit(solution)/shard_map/pallas_call | solution.py:357
  10.4 1.8 %collective-permute-start = (f32[8,16,128]{2,1,0:T(8,128)S(1)}, f32[8,16,128]{2,1,0:T(8,128)S(1)}, u32[]{:S(2)}, u32[]{:S(2)}) collective-permute-start(f32[8,16,128]{2,1,0:T(8,128)S(1)} %get-tuple-element.21), channel_id=1, source_target_pairs={{0,2},{1,3},{2,0},{3,1},{4,6},{5,7},{6,4},{7,5},{8,10},{9,11},{10,... | collective-permute-start | bytes 196616 | tf_op jit(solution)/shard_map/ppermute | solution.py:273
  12.3 1.5 %shard_map.101 = (bf16[256,512]{1,0:T(8,128)(2,1)S(1)}, s32[1,512]{1,0:T(1,128)S(1)}, s32[4,4]{1,0:T(4,128)S(4)}, s32[4]{0:T(128)S(4)}, bf16[4,4,3,128,128]{4,3,2,1,0:T(8,128)(2,1)S(1)}) custom-call(bf16[768,128]{1,0:T(8,128)(2,1)} %shard_map.100.after_ref, s32[1,512]{1,0:T(1,128)} %map_hbm.3, s32[4,4]{1,0:T(4,128)} %refs_0_.1, s32[4]{0:T(128)} %refs_1_.1, ...), custom_call_target="tpu_custom_call" | custom-call | bytes 3000000 | tf_op jit(solution)/shard_map/pallas_call | solution.py:373
  13.7 2.0 %collective-permute-done.refs_1_ = f32[8,16,128]{2,1,0:T(8,128)S(1)} collective-permute-done((f32[8,16,128]{2,1,0:T(8,128)S(1)}, f32[8,16,128]{2,1,0:T(8,128)S(1)}, u32[]{:S(2)}, u32[]{:S(2)}) %collective-permute-start) | collective-permute-done | bytes 65568 | tf_op jit(solution)/shard_map/ppermute | solution.py:273
  15.7 3.0 %all-to-all-done = bf16[32,24,128]{2,1,0:T(8,128)(2,1)S(1)} async-done(((bf16[32,24,128]{2,1,0:T(8,128)(2,1)}), bf16[32,24,128]{2,1,0:T(8,128)(2,1)S(1)}, u32[]{:S(2)}, u32[]{:S(2)}) %all-to-all-start) | async-done | bytes 196640 | tf_op jit(solution)/shard_map/all_to_all | solution.py:390
  18.7 0.8 %shard_map.103 = (bf16[2,12,16,128]{3,2,1,0:T(8,128)(2,1)S(1)}, bf16[2,256,256]{2,1,0:T(8,128)(2,1)S(1)}, f32[2,4,16,128]{3,2,1,0:T(8,128)S(1)}) custom-call(bf16[256,512]{1,0:T(8,128)(2,1)S(1)} %get-tuple-element.18.after_ref.moves_ref, bf16[768,128]{1,0:T(8,128)(2,1)S(1)} %bitcast.4, f32[8,16,128]{2,1,0:T(8,128)S(1)} %get-tuple-element.20.refs_0_, ...), custom_call_target="tpu_custom_call" | custom-call | flops 536870912 | tf_op jit(solution)/shard_map/pallas_call | solution.py:403
  19.5 0.1 collective-permute-start.1
  19.6 0.7 %shard_map.104.refs_0_ = bf16[2,12,16,128]{3,2,1,0:T(8,128)(2,1)S(1)} custom-call(bf16[2,256,256]{2,1,0:T(8,128)(2,1)S(1)} %get-tuple-element.22.tables, f32[2,4,16,128]{3,2,1,0:T(8,128)S(1)} %get-tuple-element.23.owns, f32[8,16,128]{2,1,0:T(8,128)S(1)} %get-tuple-element.20.refs_0_, f32[8,16,128]{2,1,0:T(8,128)S(1)} %collective-permute-done.refs_1_), custom_call_target="tpu_custom_call" | custom-call | flops 536870912 | bytes 4000000 | tf_op jit(solution)/shard_map/pallas_call | solution.py:410
  20.4 0.5 %collective-permute-done.1.refs_1_ = bf16[2,12,16,128]{3,2,1,0:T(8,128)(2,1)S(1)} collective-permute-done((bf16[2,12,16,128]{3,2,1,0:T(8,128)(2,1)S(1)}, bf16[2,12,16,128]{3,2,1,0:T(8,128)(2,1)S(1)}, u32[]{:S(2)}, u32[]{:S(2)}) %collective-permute-start.1) | collective-permute-done | bytes 98336 | tf_op jit(solution)/shard_map/ppermute | solution.py:273
  20.9 0.7 %shard_map.105 = f32[8,8,128]{2,1,0:T(8,128)S(1)} custom-call(s32[4,4]{1,0:T(4,128)S(4)} %get-tuple-element.15.cover_ref, s32[4]{0:T(128)S(4)} %get-tuple-element.16.count_ref, bf16[4,4,3,128,128]{4,3,2,1,0:T(8,128)(2,1)S(1)} %get-tuple-element.17.weight_ref, bf16[256,512]{1,0:T(8,128)(2,1)S(1)} %get-tuple-element.18.after_ref.moves_ref, ...), custom_call_target="tpu_custom_call" | custom-call | tf_op jit(solution)/shard_map/pallas_call | solution.py:422
  21.6 8.3 %all_to_all.16 = f32[8,8,128]{2,0,1:T(8,128)S(1)} all-to-all(f32[8,8,128]{2,0,1:T(8,128)S(1)} %bitcast.5), channel_id=1, replica_groups={{16,12,20,8,24,4,28,0},{17,13,21,9,25,5,29,1},{18,14,22,10,26,6,30,2},{..., dimensions={1} | all-to-all | bytes 65536 | tf_op jit(solution)/shard_map/all_to_all | solution.py:283
  29.9 0.7 %shard_map.106 = f32[12,512]{1,0:T(8,128)} custom-call(f32[8,8,128]{2,1,0:T(8,128)S(1)} %bitcast.6), custom_call_target="tpu_custom_call" | custom-call | tf_op jit(solution)/shard_map/pallas_call | solution.py:430
Async XLA Ops:
  2.1 16.6 %all-to-all-start = ((bf16[32,24,128]{2,1,0:T(8,128)(2,1)}), bf16[32,24,128]{2,1,0:T(8,128)(2,1)S(1)}, u32[]{:S(2)}, u32[]{:S(2)}) async-start(bf16[32,24,128]{2,1,0:T(8,128)(2,1)} %bitcast), calls=%async_computation | async-start | bytes 393216 | tf_op jit(solution)/shard_map/all_to_all | solution.py:390
  10.4 5.3 %collective-permute-start = (f32[8,16,128]{2,1,0:T(8,128)S(1)}, f32[8,16,128]{2,1,0:T(8,128)S(1)}, u32[]{:S(2)}, u32[]{:S(2)}) collective-permute-start(f32[8,16,128]{2,1,0:T(8,128)S(1)} %get-tuple-element.21), channel_id=1, source_target_pairs={{0,2},{1,3},{2,0},{3,1},{4,6},{5,7},{6,4},{7,5},{8,10},{9,11},{10,... | collective-permute-start | bytes 196616 | tf_op jit(solution)/shard_map/ppermute | solution.py:273
  19.5 1.4 %collective-permute-start.1 = (bf16[2,12,16,128]{3,2,1,0:T(8,128)(2,1)S(1)}, bf16[2,12,16,128]{3,2,1,0:T(8,128)(2,1)S(1)}, u32[]{:S(2)}, u32[]{:S(2)}) collective-permute-start(bf16[2,12,16,128]{3,2,1,0:T(8,128)(2,1)S(1)} %get-tuple-element.24), channel_id=1, source_target_pairs={{0,1},{1,0},{2,3},{3,2},{4,5},{5,4},{6,7},{7,6},{8,9},{9,8},{10,11... | collective-permute-start | bytes 294920 | tf_op jit(solution)/shard_map/ppermute | solution.py:273
